TPU v7x, 256 devices: a whole 4x4x8 slice. The times are simulated.
256 devices in a mesh: ctx: 16 (over z_hi, x), exp: 8 (over y, z_lo), dp: 2 (over core).
Axes of the slice: x: 4, y: 4, z: 8 (z_hi: 4, z_lo: 2; z = z_hi * 2 + z_lo), core: 2. Of those that a mesh axis runs over, the one named last changes fastest.
Arguments:
- query: bfloat16 [2, 2048, 10240], P('dp', 'ctx', 'exp'), may hold values from -6 to 6
- key_rows: bfloat16 [2, 4096, 1024], P('dp', 'ctx', 'exp'), may hold values from -6 to 6
- value_rows: bfloat16 [2, 4096, 1024], P('dp', 'ctx', 'exp'), may hold values from -6 to 6
- out_grad: bfloat16 [2, 2048, 10240], P('dp', 'ctx', 'exp'), may hold values from -6 to 6
- block_offsets: int32 [16], replicated, may hold values from 0 to 15, each once
- tok_grad: bfloat16 [32768, 6400], P(('ctx', 'exp', 'dp')), may hold values from -0.75 to 0.75
- hidden_act: bfloat16 [32768, 640], P(('ctx', 'exp', 'dp')), may hold values from -6 to 6
- router_prob: bfloat16 [32768], P(('ctx', 'exp', 'dp')), may hold values from 0.19921875 to 1
- expert_ids: int32 [32768, 1], P(('ctx', 'exp', 'dp')), may hold values from 0 to 7; in each aligned block of 128 rows (0 to 127, 128 to 255, ...) at most 24 rows name the same one
- down_weight: bfloat16 [8, 6400, 640], P('exp', ('ctx', 'dp')), may hold values from -0.25 to 0.25
Outputs:
- query_grad: bfloat16 [2, 2048, 10240], P('dp', 'ctx', 'exp')
- key_grad: bfloat16 [2, 4096, 1024], P('dp', 'ctx', 'exp')
- value_grad: bfloat16 [2, 4096, 1024], P('dp', 'ctx', 'exp')
- hidden_grad: bfloat16 [32768, 640], P(('ctx', 'exp', 'dp'))
- route_grad: bfloat16 [32768], P(('ctx', 'exp', 'dp'))
- weight_grad: bfloat16 [8, 6400, 640], P('exp', ('ctx', 'dp'))
Inputs may be any that keep to these rules, and one draw needn't show every extreme that they name: `expert_ids`: within the 128 rows of one device no expert is named by more than 24 rows. `block_offsets`: each block number appears once.
All inputs are finite; a program needn't handle non-finite values.
Results may differ from a plain program's by a relative error of at most 0.025.
Values may be sent and summed in bfloat16 or wider, within the bound.
A program may use at most 128 MiB of HBM per device.

v0:
```python
import math

import jax
import jax.numpy as jnp
from jax import lax
from jax.sharding import PartitionSpec as P

HD = 128
GROUP = 10


NEG_FILL = -1e30


def over_blocks(advance, running, key_block, value_block, offset):
    key_count = key_block.shape[0]
    block_len = 512
    turn_total = key_count // block_len

    def one_turn(turn_index, current):
        shift_by = turn_index * block_len
        part_keys = lax.dynamic_slice_in_dim(key_block, shift_by, block_len, 0)
        part_values = lax.dynamic_slice_in_dim(value_block, shift_by, block_len, 0)
        return advance(current, part_keys, part_values, offset + shift_by)

    return lax.fori_loop(0, turn_total, one_turn, running)


def per_device(
    query,
    key_rows,
    value_rows,
    out_grad,
    block_offsets,
    tok_grad,
    hidden_act,
    router_prob,
    expert_ids,
    down_weight,
):
    query_rows = query.shape[1]
    key_count = key_rows.shape[1]
    ctx_size = lax.axis_size("ctx")
    ctx_index = lax.axis_index("ctx")
    window = key_count * ctx_size
    inv_root = 1.0 / math.sqrt(HD)
    own_offset = lax.dynamic_index_in_dim(block_offsets, ctx_index, keepdims=False)
    query_pos = (
        own_offset * key_count + (key_count - query_rows) + jnp.arange(query_rows, dtype=jnp.int32)
    )
    queries = query[0].reshape(query_rows, GROUP, HD)
    grads_out = out_grad[0].reshape(query_rows, GROUP, HD)
    block_ids = jnp.arange(ctx_size, dtype=jnp.int32)

    def key_positions(offset, key_total):
        rows_at = offset + jnp.arange(key_total, dtype=jnp.int32)
        owner = (rows_at // key_count)[:, None] == block_ids[None, :]
        return (
            jnp.sum(jnp.where(owner, block_offsets[None, :], 0), axis=1) * key_count
            + rows_at % key_count
        )

    def scored(key_block, offset):
        scores = (
            jnp.einsum("qhd,kd->hqk", queries, key_block, preferred_element_type=jnp.float32)
            * inv_root
        )
        positions = key_positions(offset, key_block.shape[0])
        visible = positions[None, :] <= query_pos[:, None]
        return (scores, visible[None])

    def first_step(running, key_block, value_block, offset):
        run_peak, run_total, run_out = running
        scores, visible = scored(key_block, offset)
        new_peak = jnp.maximum(run_peak, jnp.max(jnp.where(visible, scores, NEG_FILL), axis=2))
        unnormed = jnp.where(
            visible, jnp.exp(jnp.where(visible, scores - new_peak[..., None], 0.0)), 0.0
        )
        rescale = jnp.exp(run_peak - new_peak)
        run_total = run_total * rescale + jnp.sum(unnormed, axis=2)
        run_out = run_out * rescale[..., None] + jnp.einsum(
            "hqk,kd->hqd",
            unnormed,
            value_block.astype(jnp.float32),
            precision=lax.Precision.HIGHEST,
        )
        return (new_peak, run_total, run_out)

    first_state = (
        jnp.full((GROUP, query_rows), NEG_FILL, jnp.float32),
        jnp.zeros((GROUP, query_rows), jnp.float32),
        jnp.zeros((GROUP, query_rows, HD), jnp.float32),
    )
    gathered = (
        lax.all_gather(key_rows[0], "ctx", axis=0, tiled=True),
        lax.all_gather(value_rows[0], "ctx", axis=0, tiled=True),
    )
    row_peak, row_total, run_out = over_blocks(first_step, first_state, gathered[0], gathered[1], 0)
    attn_out = run_out / row_total[..., None]
    row_delta = jnp.sum(grads_out.transpose(1, 0, 2).astype(jnp.float32) * attn_out, axis=2)

    def second_step(running, key_block, value_block, offset):
        query_acc, key_acc, value_acc = running
        scores, visible = scored(key_block, offset)
        softmaxed = (
            jnp.where(visible, jnp.exp(jnp.where(visible, scores - row_peak[..., None], 0.0)), 0.0)
            / row_total[..., None]
        )
        probs_low = softmaxed.astype(jnp.bfloat16)
        value_part = jnp.einsum(
            "hqk,qhd->kd", probs_low, grads_out, preferred_element_type=jnp.float32
        )
        prob_grad = jnp.einsum(
            "qhd,kd->hqk", grads_out, value_block, preferred_element_type=jnp.float32
        )
        score_grad = (softmaxed * (prob_grad - row_delta[..., None])).astype(jnp.bfloat16)
        query_acc = query_acc + jnp.einsum(
            "hqk,kd->hqd", score_grad, key_block, preferred_element_type=jnp.float32
        )
        key_part = (
            jnp.einsum("hqk,qhd->kd", score_grad, queries, preferred_element_type=jnp.float32)
            * inv_root
        )
        size_now = key_block.shape[0]
        key_acc = lax.dynamic_update_slice_in_dim(
            key_acc, lax.dynamic_slice_in_dim(key_acc, offset, size_now, 0) + key_part, offset, 0
        )
        value_acc = lax.dynamic_update_slice_in_dim(
            value_acc,
            lax.dynamic_slice_in_dim(value_acc, offset, size_now, 0) + value_part,
            offset,
            0,
        )
        return (query_acc, key_acc, value_acc)

    second_state = (
        jnp.zeros((GROUP, query_rows, HD), jnp.float32),
        jnp.zeros((window, HD), jnp.float32),
        jnp.zeros((window, HD), jnp.float32),
    )
    query_acc, key_acc, value_acc = over_blocks(
        second_step, second_state, gathered[0], gathered[1], 0
    )
    key_total, value_total = (
        lax.psum_scatter(
            key_acc.astype(jnp.bfloat16), "ctx", scatter_dimension=0, tiled=True
        ).astype(jnp.float32),
        lax.psum_scatter(
            value_acc.astype(jnp.bfloat16), "ctx", scatter_dimension=0, tiled=True
        ).astype(jnp.float32),
    )
    query_grad = (
        (query_acc * inv_root)
        .transpose(1, 0, 2)
        .reshape(1, query_rows, GROUP * HD)
        .astype(jnp.bfloat16)
    )
    key_grad = key_total.astype(jnp.bfloat16)[None]
    value_grad = value_total.astype(jnp.bfloat16)[None]
    tok_count = tok_grad.shape[0]
    exp_size = lax.axis_size("exp")
    capacity = 3 * tok_count // (2 * exp_size)
    model_width = tok_grad.shape[1]
    hidden_width = hidden_act.shape[1]
    route_ids = expert_ids[:, 0]
    choose = (route_ids[:, None] == jnp.arange(exp_size, dtype=jnp.int32)[None, :]).astype(
        jnp.int32
    )
    slot_rank = jnp.sum((jnp.cumsum(choose, axis=0) - 1) * choose, axis=1)
    target = route_ids * capacity + slot_rank
    slot_total = exp_size * capacity
    send_grad = (
        jnp.zeros((slot_total, model_width), jnp.bfloat16)
        .at[target]
        .set(tok_grad)
        .reshape(exp_size, capacity, model_width)
    )
    send_act = (
        jnp.zeros((slot_total, hidden_width), jnp.bfloat16)
        .at[target]
        .set(hidden_act)
        .reshape(exp_size, capacity, hidden_width)
    )
    send_prob = (
        jnp.zeros((slot_total,), jnp.bfloat16)
        .at[target]
        .set(router_prob)
        .reshape(exp_size, capacity)
    )
    got_grad, got_act, got_prob = (
        lax.all_to_all(send_grad, "exp", split_axis=0, concat_axis=0, tiled=True),
        lax.all_to_all(send_act, "exp", split_axis=0, concat_axis=0, tiled=True),
        lax.all_to_all(send_prob, "exp", split_axis=0, concat_axis=0, tiled=True),
    )
    recv_grad = got_grad.reshape(slot_total, model_width)
    recv_act = got_act.reshape(slot_total, hidden_width)
    recv_prob = got_prob.reshape(slot_total).astype(jnp.float32)
    weight_rows = lax.all_gather(down_weight, ("ctx", "dp"), axis=1, tiled=True)[0]
    grad_cols = recv_grad
    hidden_acc = jnp.dot(grad_cols, weight_rows, preferred_element_type=jnp.float32)
    expert_out = lax.dot_general(
        recv_act, weight_rows, (((1,), (1,)), ((), ())), preferred_element_type=jnp.float32
    )
    route_acc = jnp.sum(grad_cols.astype(jnp.float32) * expert_out, axis=1)
    hidden_acc, route_acc = (hidden_acc, route_acc)
    hidden_back = (
        (recv_prob[:, None] * hidden_acc)
        .astype(jnp.bfloat16)
        .reshape(exp_size, capacity, hidden_width)
    )
    route_back = route_acc.astype(jnp.bfloat16).reshape(exp_size, capacity)
    back_hidden, back_route = (
        lax.all_to_all(hidden_back, "exp", split_axis=0, concat_axis=0, tiled=True),
        lax.all_to_all(route_back, "exp", split_axis=0, concat_axis=0, tiled=True),
    )
    hidden_grad = back_hidden.reshape(slot_total, hidden_width)[target]
    route_grad = back_route.reshape(slot_total)[target]
    scaled_grad = (recv_prob[:, None] * recv_grad.astype(jnp.float32)).astype(jnp.bfloat16)
    grad_cols = scaled_grad
    weight_total = lax.psum_scatter(
        lax.dot_general(
            grad_cols, recv_act, (((0,), (0,)), ((), ())), preferred_element_type=jnp.float32
        ).astype(jnp.bfloat16),
        ("ctx", "dp"),
        scatter_dimension=0,
        tiled=True,
    )
    weight_grad = weight_total[None]
    return (query_grad, key_grad, value_grad, hidden_grad, route_grad, weight_grad)


def solution(mesh):
    in_specs = (
        P("dp", "ctx", "exp"),
        P("dp", "ctx", "exp"),
        P("dp", "ctx", "exp"),
        P("dp", "ctx", "exp"),
        P(),
        P(("ctx", "exp", "dp"), None),
        P(("ctx", "exp", "dp"), None),
        P(("ctx", "exp", "dp")),
        P(("ctx", "exp", "dp"), None),
        P("exp", ("ctx", "dp"), None),
    )
    out_specs = (
        P("dp", "ctx", "exp"),
        P("dp", "ctx", "exp"),
        P("dp", "ctx", "exp"),
        P(("ctx", "exp", "dp"), None),
        P(("ctx", "exp", "dp")),
        P("exp", ("ctx", "dp"), None),
    )
    return jax.shard_map(
        per_device, mesh=mesh, in_specs=in_specs, out_specs=out_specs, check_vma=False
    )
```

profile of v0, /device:TPU:81, one launch (start us, length us, event | category | flops | bytes accessed | tf_op | source)
XLA Modules:
  0.0 583.5 jit_solution(8869063398588245482)
XLA Ops:
  13.2 5.6 all-to-all-start
  22.4 5.5 scatter_custom_fusion.1
  27.9 2.2 scatter_custom_fusion.2
  31.3 5.2 all-to-all-start.3
  36.5 26.2 %all-gather.8.cloned.1.call-done = bf16[1,4096,128]{2,1,0:T(8,128)(2,1)} async-done(((bf16[1,256,128]{2,1,0:T(8,128)(2,1)}), bf16[1,4096,128]{2,1,0:T(8,128)(2,1)}) %all-gather.8.cloned.1.call-update) | async-done | bytes 1048592 | tf_op jit(solution)/shard_map/all_gather | solution.py:95
  62.7 53.2 %all-gather.10.cloned.1.call-done = bf16[1,4096,128]{2,1,0:T(8,128)(2,1)} async-done(((bf16[1,256,128]{2,1,0:T(8,128)(2,1)}), bf16[1,4096,128]{2,1,0:T(8,128)(2,1)}) %all-gather.10.cloned.1.call-update) | async-done | bytes 1048592 | tf_op jit(solution)/shard_map/all_gather | solution.py:96
  115.9 57.8 %while.40 = (s32[]{:T(128)}, f32[10,128]{1,0:T(8,128)S(1)}, f32[10,128]{1,0:T(8,128)S(1)}, f32[10,128,128]{2,1,0:T(8,128)}, s32[16]{0:T(128)S(1)}, /*index=5*/bf...) while((s32[]{:T(128)}, f32[10,128]{1,0:T(8,128)S(1)}, ...), condition=%wide.region_4.5_spmd.clone, body=%wide.region_0.4_spmd.clone.sunk | while | flops 1182872448 | bytes 15365443 | solution.py:26
  118.7 3.5 fusion.131
  126.0 3.5 fusion.131
  133.2 3.5 fusion.131
  140.4 3.5 fusion.131
  147.7 3.5 fusion.131
  154.9 3.5 fusion.131
  162.1 3.5 fusion.131
  169.3 3.5 fusion.131
  176.2 5.5 all-to-all-start.1
  184.7 76.1 %while.41 = (s32[]{:T(128)}, f32[10,128,128]{2,1,0:T(8,128)S(1)}, f32[4096,128]{1,0:T(8,128)}, f32[4096,128]{1,0:T(8,128)}, s32[16]{0:T(128)S(1)}, /*index=5*/bf...) while((s32[]{:T(128)}, f32[10,128,128]{2,1,0:T(8,128)S(1)}, ...), condition=%wide.region_8.9_spmd.clone, body=%wide.region_6.8_spmd.clone.sunk | while | flops 845388416 | bytes 16019765 | solution.py:26
  188.2 2.2 fusion.145
  190.3 2.2 fusion.146
  194.5 1.7 fusion.143
  197.7 2.2 fusion.145
  199.9 2.2 fusion.146
  204.0 1.7 fusion.143
  207.2 2.2 fusion.145
  209.4 2.2 fusion.146
  216.8 2.2 fusion.145
  218.9 2.2 fusion.146
  223.1 1.7 fusion.143
  226.3 2.2 fusion.145
  228.4 2.2 fusion.146
  235.8 2.2 fusion.145
  237.9 2.2 fusion.146
  242.1 1.7 fusion.143
  245.3 2.2 fusion.145
  247.4 2.2 fusion.146
  251.6 1.7 fusion.143
  254.8 2.2 fusion.145
  256.9 2.2 fusion.146
  260.8 2.7 convert_element_type.111
  263.6 2.7 convert_element_type.112
  266.3 7.8 %bitcast_convert_fusion = bf16[6400,640]{1,0:T(8,128)(2,1)} fusion(bf16[8,24,640]{2,1,0:T(8,128)(2,1)} %all-to-all-done.3, bf16[8,24,6400]{2,1,0:T(8,128)(2,1)} %all-to-all-done.1, f32[8,24]{1,0:T(8,128)S(1)} %bitcast.160), kind=kOutput, calls=%fused_computation.93 | convolution fusion | flops 1580646400 | bytes 10896128 | tf_op jit(solution)/shard_map/dot_general | solution.py:221
  274.2 6.9 %fusion.73 = bf16[192]{0:T(256)(128)(2,1)S(1)} fusion(bf16[192,640]{1,0:T(8,128)(2,1)} %bitcast.19, bf16[1,6400,640]{2,1,0:T(8,128)(2,1)} %all-gather.6.cloned.1.call-done, bf16[192,6400]{1,0:T(8,128)(2,1)} %bitcast.14), kind=kOutput, calls=%fused_computation.100 | convolution fusion | flops 1576550144 | bytes 10895744 | tf_op jit(solution)/shard_map/dot_general | solution.py:201
  281.8 5.1 all-to-all-start.4
  287.0 6.9 %fusion.81 = bf16[192,640]{1,0:T(8,128)(2,1)} fusion(bf16[192,6400]{1,0:T(8,128)(2,1)} %bitcast.14, bf16[1,6400,640]{2,1,0:T(8,128)(2,1)} %all-gather.6.cloned.1.call-done, f32[192]{0:T(256)S(1)} %reshape.237), kind=kOutput, calls=%fused_computation.104 | convolution fusion | flops 1573109760 | bytes 10896128 | tf_op jit(solution)/shard_map/dot_general | solution.py:200
  293.8 5.1 all-to-all-start.2
  305.0 42.4 %reduce-scatter.6.cloned.1.call-done = bf16[256,128]{1,0:T(8,128)(2,1)} async-done(((bf16[4096,128]{1,0:T(8,128)(2,1)}), bf16[256,128]{1,0:T(8,128)(2,1)}) %reduce-scatter.6.cloned.1.call-update) | async-done | bytes 65552 | tf_op jit(solution)/shard_map/reduce_scatter | solution.py:145
  347.4 88.3 %reduce-scatter.8.cloned.1.call-done = bf16[256,128]{1,0:T(8,128)(2,1)} async-done(((bf16[4096,128]{1,0:T(8,128)(2,1)}), bf16[256,128]{1,0:T(8,128)(2,1)}) %reduce-scatter.8.cloned.1.call-update) | async-done | bytes 65552 | tf_op jit(solution)/shard_map/reduce_scatter | solution.py:148
  435.7 140.9 %reduce-scatter.10.cloned.1.call-done = bf16[200,640]{1,0:T(8,128)(2,1)} async-done(((bf16[6400,640]{1,0:T(8,128)(2,1)}), bf16[200,640]{1,0:T(8,128)(2,1)}) %reduce-scatter.10.cloned.1.call-update) | async-done | bytes 256016
  (226 shorter events, 83.6 us)
Async XLA Ops:
  7.2 55.5 %all-gather.8.cloned.1.call-start = ((), (), s32[]{:S(2)}) async-start(), calls=%async_computation.11 | async-start | bytes 1114112 | tf_op jit(solution)/shard_map/all_gather | solution.py:95
  7.9 108.0 %all-gather.10.cloned.1.call-start = ((), (), s32[]{:S(2)}) async-start(), calls=%async_computation.12 | async-start | bytes 1114112 | tf_op jit(solution)/shard_map/all_gather | solution.py:96
  13.2 18.1 %all-to-all-start = ((bf16[8,1,24]{2,1,0:T(2,128)(2,1)}), bf16[8,1,24]{2,1,0:T(2,128)(2,1)S(1)}, u32[]{:S(2)}, u32[]{:S(2)}) async-start(bf16[8,1,24]{2,1,0:T(2,128)(2,1)} %all_to_all.25), calls=%async_computation.2 | async-start | bytes 8192 | tf_op jit(solution)/shard_map/all_to_all | solution.py:193
  18.8 255.4 %all-gather.6.cloned.1.call-start = ((), (), s32[]{:S(2)}) async-start(), calls=%async_computation.10 | async-start | bytes 8448000 | tf_op jit(solution)/shard_map/all_gather | solution.py:198
  19.6 10.5 %copy-start.4 = (s32[16]{0:T(128)S(1)}, s32[16]{0:T(128)}, u32[]{:S(2)}) copy-start(s32[16]{0:T(128)} %param.18) | copy-start | bytes 196
  22.2 93.7 %copy-start.1 = (bf16[1,128,1280]{1,2,0:T(8,128)(2,1)}, bf16[1,128,1280]{1,2,0:T(8,128)(2,1)S(1)}, u32[]{:S(2)}) copy-start(bf16[1,128,1280]{1,2,0:T(8,128)(2,1)S(1)} %copy.56) | copy-start | bytes 983044
  31.3 144.9 %all-to-all-start.3 = ((bf16[8,24,640]{2,1,0:T(8,128)(2,1)}), bf16[8,24,640]{2,1,0:T(8,128)(2,1)}, u32[]{:S(2)}, u32[]{:S(2)}) async-start(bf16[8,24,640]{2,1,0:T(8,128)(2,1)} %bitcast.18), calls=%async_computation.5 | async-start | bytes 491520 | tf_op jit(solution)/shard_map/all_to_all | solution.py:192
  117.6 1.1 copy-start.2
  122.3 0.9 copy-start.3
  124.9 1.1 copy-start.2
  129.5 0.9 copy-start.3
  132.1 1.1 copy-start.2
  136.7 0.9 copy-start.3
  139.3 1.1 copy-start.2
  144.0 0.9 copy-start.3
  146.6 1.1 copy-start.2
  151.2 0.9 copy-start.3
  153.8 1.1 copy-start.2
  158.4 0.9 copy-start.3
  161.0 1.1 copy-start.2
  165.6 0.9 copy-start.3
  168.3 1.1 copy-start.2
  172.9 0.9 copy-start.3
  176.2 90.1 %all-to-all-start.1 = ((bf16[8,24,6400]{2,1,0:T(8,128)(2,1)}), bf16[8,24,6400]{2,1,0:T(8,128)(2,1)}, u32[]{:S(2)}, u32[]{:S(2)}) async-start(bf16[8,24,6400]{2,1,0:T(8,128)(2,1)} %bitcast.154), calls=%async_computation.3 | async-start | bytes 4915200 | tf_op jit(solution)/shard_map/all_to_all | solution.py:191
  181.8 3.0 copy-start
  181.8 165.6 %reduce-scatter.6.cloned.1.call-start = ((), (), s32[]{:S(2)}) async-start(), calls=%async_computation.8 | async-start | bytes 1114112 | tf_op jit(solution)/shard_map/reduce_scatter | solution.py:145
  263.5 172.2 %reduce-scatter.8.cloned.1.call-start = ((), (), s32[]{:S(2)}) async-start(), calls=%async_computation.9 | async-start | bytes 1114112 | tf_op jit(solution)/shard_map/reduce_scatter | solution.py:148
  266.3 310.4 %reduce-scatter.10.cloned.1.call-start = ((), (), s32[]{:S(2)}) async-start(), calls=%async_computation.13 | async-start | bytes 8448000
  281.8 12.0 %all-to-all-start.4 = ((bf16[8,1,24]{2,1,0:T(2,128)(2,1)}), bf16[8,1,24]{2,1,0:T(2,128)(2,1)S(1)}, u32[]{:S(2)}, u32[]{:S(2)}) async-start(bf16[8,1,24]{2,1,0:T(2,128)(2,1)} %convert_element_type.130), calls=%async_computation.6 | async-start | bytes 8192 | tf_op jit(solution)/shard_map/all_to_all | solution.py:214
  293.8 9.6 %all-to-all-start.2 = ((bf16[8,24,640]{2,1,0:T(8,128)(2,1)}), bf16[8,24,640]{2,1,0:T(8,128)(2,1)S(1)}, u32[]{:S(2)}, u32[]{:S(2)}) async-start(bf16[8,24,640]{2,1,0:T(8,128)(2,1)} %bitcast.16), calls=%async_computation.4 | async-start | bytes 491520 | tf_op jit(solution)/shard_map/all_to_all | solution.py:213
Sparse Core Ops, SparseCore 0:
  10.4 52.2 all-gather.7
  65.1 50.7 all-gather.9
  118.6 78.0 all-gather.5
  263.6 83.6 reduce-scatter.5
  351.7 83.9 reduce-scatter.7
  440.3 136.2 reduce-scatter.9
where the time goes:
time: 589 us; the launch traced here: 583 us
  waiting for transfers between devices  355 us (60%)
  matrix products  135 us (23%)
  local copies, waits for them, and re-layouts  33 us (6%)
  starting transfers between devices  26.7 us (5%)
  other arithmetic  18.2 us (3%)
  between operations  14.9 us (3%)
    unnamed x7, waiting for transfers between devices  143 us
    reduce_scatter x1, waiting for transfers between devices, per_device(): lax.psum_scatter(value_acc.astype(jnp.bfloat16), 'ctx', scatter_dimension...  88.3 us
    all_gather x1, waiting for transfers between devices, per_device(): lax.all_gather(value_rows[0], 'ctx', axis=0, tiled=True)  53.2 us
    reduce_scatter x1, waiting for transfers between devices, per_device(): lax.psum_scatter(key_acc.astype(jnp.bfloat16), 'ctx', scatter_dimension=0...  42.4 us
    dot_general x8, matrix products, first_step(): jnp.einsum('hqk,kd->hqd', unnormed, value_block.astype(jnp.float32), prec...  28.2 us
    all_gather x1, waiting for transfers between devices, per_device(): lax.all_gather(key_rows[0], 'ctx', axis=0, tiled=True)  26.2 us
    dot_general x16, matrix products, scored(): jnp.einsum('qhd,kd->hqk', queries, key_block, preferred_element_type=jnp....  25.6 us
    dot_general x8, matrix products, second_step(): jnp.einsum('hqk,qhd->kd', probs_low, grads_out, preferred_element_type=jn...  17.5 us
  transfers between devices with their start and end apart: 11, of which 6 were waited for; matrix products, arithmetic and copies ran while one was open for 30% of the time, Pallas kernels for 0%

commit v1 on v0

v1 whole, which is shorter than its diff:
```python
import math

import jax
import jax.numpy as jnp
from jax import lax
from jax.experimental import pallas as pl
from jax.experimental.pallas import tpu as pltpu
from jax.sharding import PartitionSpec as P

HD = 128
GROUP = 10
NEG_FILL = -1e30
MESH = pl.DeviceIdType.MESH
F32 = jnp.float32
BF16 = jnp.bfloat16

NX, NZ, NE, ND = 4, 4, 8, 2
KEYS = 256
QRY = 128
COLS = GROUP * QRY
TOK = 128
CAP = 24
D = 6400
HALF = D // 2
FF = 640
PART = (HALF + FF) // 2
WB = 400
WS = 200
WP = 208
SLOTS = NE * CAP
ROWS = ND * SLOTS

NT = (((1,), (1,)), ((), ()))
TN = (((0,), (0,)), ((), ()))


def dot(a, b, dims=(((1,), (0,)), ((), ()))):
    return lax.dot_general(a, b, dims, preferred_element_type=F32)


def kernel(
    off_ref,
    q_ref,
    k_ref,
    v_ref,
    do_ref,
    tok_ref,
    act_ref,
    prob_ref,
    idr_ref,
    idc_ref,
    w_ref,
    dq_out,
    dk_out,
    dv_out,
    hid_out,
    route_out,
    dw_out,
    kv,
    qs,
    dos,
    stat_m,
    stat_l,
    stat_d,
    p_buf,
    ds_buf,
    dq_acc,
    dkv,
    dkv_x,
    dkv_zs,
    dkv_zr,
    perm,
    tsend,
    trecv,
    gbuf,
    abuf,
    wpad,
    wraw,
    wfull,
    wg,
    wg_x,
    wg_zs,
    wg_zr,
    hsend,
    hrecv,
    kz_s,
    kz_r,
    kx_s,
    kx_r,
    wz_s,
    wz_r,
    wx_s,
    wx_r,
    tk_s,
    tk_r,
    dx_s,
    dx_r,
    dz_s,
    dz_r,
    gx_s,
    gx_r,
    gz_s,
    gz_r,
    hb_s,
    hb_r,
):
    ctx = lax.axis_index("ctx")
    exp = lax.axis_index("exp")
    core = lax.axis_index("dp")
    z = ctx // NX
    x = ctx % NX
    inv_root = 1.0 / math.sqrt(HD)
    scale2 = inv_root * math.log2(math.e)

    def xpeer(dx):
        return lax.rem(x + dx, NX)

    def zpeer(dz):
        return lax.rem(z + dz, NZ)

    def remote(src, dst, ss, rs, dev):
        return pltpu.make_async_remote_copy(
            src_ref=src, dst_ref=dst, send_sem=ss, recv_sem=rs, device_id=dev, device_id_type=MESH
        )

    barrier = pltpu.get_barrier_semaphore()
    count = 0
    for dx in range(1, NX):
        pl.semaphore_signal(
            barrier, inc=1, device_id=(z * NX + xpeer(dx), exp, core), device_id_type=MESH
        )
        count += 1
    for dz in range(0, NZ):
        for dh in range(ND):
            if dz == 0 and dh == 0:
                continue
            pl.semaphore_signal(
                barrier,
                inc=1,
                device_id=(zpeer(dz) * NX + x, exp, lax.rem(core + dh, ND)),
                device_id_type=MESH,
            )
            count += 1
    for de in range(1, NE):
        for dh in range(ND):
            pl.semaphore_signal(
                barrier,
                inc=1,
                device_id=(ctx, lax.rem(exp + de, NE), lax.rem(core + dh, ND)),
                device_id_type=MESH,
            )
            count += 1
    pl.semaphore_wait(barrier, count)

    kv[x, z, 0:KEYS] = k_ref[...]
    kv[x, z, KEYS : 2 * KEYS] = v_ref[...]

    def kz_copy(dz):
        return remote(
            kv.at[x, z],
            kv.at[x, z],
            kz_s.at[dz - 1],
            kz_r.at[dz - 1],
            (zpeer(dz) * NX + x, exp, core),
        )

    def kx_copy(dx, dz):
        zz = zpeer(NZ - dz)
        return remote(
            kv.at[x, zz],
            kv.at[x, zz],
            kx_s.at[(dx - 1) * NZ + dz],
            kx_r.at[(dx - 1) * NZ + dz],
            (z * NX + xpeer(dx), exp, core),
        )

    for dz in range(1, NZ):
        kz_copy(dz).start()
    for dx in range(1, NX):
        kx_copy(dx, 0).start()

    wpad[0:WS] = w_ref[...]
    wpad[WS:WP] = jnp.zeros((WP - WS, FF), BF16)
    w_core = z // 2
    w_slot = lax.rem(z, 2)
    w_here = core == w_core

    def wz_copy(dz):
        return remote(
            wpad,
            wraw.at[w_slot, core],
            wz_s.at[dz],
            wz_r.at[w_slot * 2 + core],
            (zpeer(dz) * NX + x, exp, w_core),
        )

    for dz in range(1, NZ):
        wz_copy(dz).start()

    @pl.when(w_here)
    def _():
        wraw[w_slot, core] = wpad[...]

    @pl.when(jnp.logical_not(w_here))
    def _():
        wz_copy(0).start()

    ids_row = idr_ref[...]
    row_at = lax.broadcasted_iota(jnp.int32, (TOK, TOK), 0)
    col_at = lax.broadcasted_iota(jnp.int32, (TOK, TOK), 1)
    same = jnp.where((idc_ref[...] == ids_row) & (row_at < col_at), 1.0, 0.0)
    rank = jnp.sum(same, axis=0, keepdims=True).astype(jnp.int32)
    target = ids_row * CAP + rank
    slot_at = lax.broadcasted_iota(jnp.int32, (SLOTS, TOK), 0)
    perm[...] = jnp.where(slot_at == target, 1.0, 0.0).astype(BF16)
    scaled_act = (prob_ref[...] * act_ref[...].astype(F32)).astype(BF16)

    def tk_copy(de, dh):
        e_to = lax.rem(exp + de, NE)
        h_to = lax.rem(core + dh, ND)
        i = de * ND + dh
        return remote(
            tsend.at[h_to, e_to],
            trecv.at[core, exp],
            tk_s.at[i],
            tk_r.at[i],
            (ctx, e_to, h_to),
        )

    for half in range(ND):
        base = half * HALF
        first = dot(perm[...], tok_ref[:, base : base + PART])
        second = dot(perm[...], tok_ref[:, base + PART : base + HALF])
        third = dot(perm[...], scaled_act)
        for e in range(NE):
            rows = slice(e * CAP, (e + 1) * CAP)
            tsend[half, e, :, 0 : HALF - PART] = jnp.concatenate(
                [first[rows, 0 : HALF - PART], second[rows]], axis=0
            ).astype(BF16)
            tsend[half, e, :, HALF - PART : PART] = jnp.concatenate(
                [first[rows, HALF - PART : PART], third[rows]], axis=0
            ).astype(BF16)
    for de in range(NE):
        for dh in range(ND):
            if de == 0 and dh == 0:
                trecv[core, exp] = tsend[core, exp]
            else:
                tk_copy(de, dh).start()

    for h in range(GROUP):
        qs[h * QRY : (h + 1) * QRY] = q_ref[:, h * HD : (h + 1) * HD]
        dos[h * QRY : (h + 1) * QRY] = do_ref[:, h * HD : (h + 1) * HD]

    for dz in range(1, NZ):
        kz_copy(dz).wait_recv()
        for dx in range(1, NX):
            kx_copy(dx, dz).start()

    def wx_copy(dx, s):
        at = pl.ds(pl.multiple_of((s * NX + x) * WB, WB), WB)
        return remote(
            wfull.at[at],
            wfull.at[at],
            wx_s.at[(dx - 1) * 2 + s],
            wx_r.at[(dx - 1) * 2 + s],
            (z * NX + xpeer(dx), exp, core),
        )

    for s in range(2):
        for h in range(ND):

            @pl.when(jnp.logical_not((2 * core + s == z) & (core == h)))
            def _():
                remote(
                    wpad, wraw.at[s, h], wz_s.at[0], wz_r.at[s * 2 + h], (ctx, exp, core)
                ).wait_recv()

        merged = jnp.concatenate(
            [wraw[s, 0, 0:WS].astype(F32), wraw[s, 1, 0:WS].astype(F32)], axis=0
        )
        wfull[pl.ds(pl.multiple_of((s * NX + x) * WB, WB), WB)] = merged.astype(BF16)
        for dx in range(1, NX):
            wx_copy(dx, s).start()

    own_pos = off_ref[ctx] * KEYS + (KEYS - QRY)
    q_pos = own_pos + lax.broadcasted_iota(jnp.int32, (KEYS, QRY), 1)
    k_at = lax.broadcasted_iota(jnp.int32, (KEYS, QRY), 0)
    wide = 2 * QRY

    def bias_of(xx, zz):
        seen = off_ref[zz * NX + xx] * KEYS + k_at <= q_pos
        one = jnp.where(seen, 0.0, NEG_FILL)
        return jnp.concatenate([one, one], axis=1)

    stat_m[...] = jnp.full((1, COLS), NEG_FILL, F32)
    stat_l[...] = jnp.zeros((1, COLS), F32)
    stat_d[...] = jnp.zeros((1, COLS), F32)

    def first_pass(xx, zz):
        bias = bias_of(xx, zz)
        keys = kv[xx, zz, 0:KEYS]
        values = kv[xx, zz, KEYS : 2 * KEYS]
        for g in range(COLS // wide):
            at = slice(g * wide, (g + 1) * wide)
            scores = dot(keys, qs[at], NT) * scale2 + bias
            grads = dot(values, dos[at], NT)
            old = stat_m[:, at]
            peak = jnp.maximum(old, jnp.max(scores, axis=0, keepdims=True))
            shrink = jnp.exp2(old - peak)
            probs = jnp.exp2(scores - peak)
            stat_m[:, at] = peak
            stat_l[:, at] = stat_l[:, at] * shrink + jnp.sum(probs, axis=0, keepdims=True)
            stat_d[:, at] = stat_d[:, at] * shrink + jnp.sum(probs * grads, axis=0, keepdims=True)

    for dx in range(NX):
        xx = xpeer(NX - dx)
        if dx:
            for dz in range(NZ):
                zz = zpeer(NZ - dz)
                remote(
                    kv.at[xx, zz],
                    kv.at[xx, zz],
                    kx_s.at[(dx - 1) * NZ + dz],
                    kx_r.at[(dx - 1) * NZ + dz],
                    (ctx, exp, core),
                ).wait_recv()

        @pl.loop(0, NZ)
        def _(zz):
            first_pass(xx, zz)

    total = stat_l[...]
    stat_m[...] = stat_m[...] + jnp.log2(total)
    stat_d[...] = stat_d[...] / total
    dq_acc[...] = jnp.zeros((HD, COLS), F32)

    def second_pass(xx, zz):
        bias = bias_of(xx, zz)
        keys = kv[xx, zz, 0:KEYS]
        values = kv[xx, zz, KEYS : 2 * KEYS]
        for g in range(COLS // wide):
            at = slice(g * wide, (g + 1) * wide)
            scores = dot(keys, qs[at], NT) * scale2 + bias
            grads = dot(values, dos[at], NT)
            probs = jnp.exp2(scores - stat_m[:, at])
            p_buf[:, at] = probs.astype(BF16)
            ds_buf[:, at] = (probs * (grads - stat_d[:, at])).astype(BF16)
        dkv[xx, zz, 0:KEYS] = (dot(ds_buf[...], qs[...]) * inv_root).astype(BF16)
        dkv[xx, zz, KEYS : 2 * KEYS] = dot(p_buf[...], dos[...]).astype(BF16)
        dq_acc[...] += dot(keys, ds_buf[...], TN)

    def dx_copy(dx):
        return remote(
            dkv.at[xpeer(dx)],
            dkv_x.at[dx - 1],
            dx_s.at[dx - 1],
            dx_r.at[dx - 1],
            (z * NX + xpeer(dx), exp, core),
        )

    for dx in (2, 1, 3, 0):
        xx = xpeer(dx)

        @pl.loop(0, NZ)
        def _(zz):
            second_pass(xx, zz)

        if dx:
            dx_copy(dx).start()

    for de in range(NE):
        for dh in range(ND):
            if de or dh:
                tk_copy(de, dh).wait_recv()

    @pl.loop(0, NE)
    def _(i):
        h = i // (NE // 2)
        e = lax.rem(i, NE // 2) * 2
        one = trecv[h, e].astype(F32)
        two = trecv[h, e + 1].astype(F32)
        at = pl.ds(pl.multiple_of(i * 2 * CAP, 2 * CAP), 2 * CAP)
        gbuf[at, 0:PART] = jnp.concatenate([one[0:CAP], two[0:CAP]], axis=0).astype(BF16)
        rest = jnp.concatenate([one[CAP:], two[CAP:]], axis=0).astype(BF16)
        gbuf[at, PART:HALF] = rest[:, 0 : HALF - PART]
        abuf[at] = rest[:, HALF - PART :]

    def gx_copy(dx, s):
        return remote(
            wg.at[pl.ds(pl.multiple_of((s * NX + xpeer(dx)) * WB, WB), WB)],
            wg_x.at[dx - 1, s],
            gx_s.at[(dx - 1) * 2 + s],
            gx_r.at[(dx - 1) * 2 + s],
            (z * NX + xpeer(dx), exp, core),
        )

    for i in range(HALF // FF):
        at = slice(i * FF, (i + 1) * FF)
        wg[at] = dot(gbuf[:, at], abuf[...], TN).astype(BF16)
        if i == 2:
            for dx in range(1, NX):
                gx_copy(dx, 0).start()
    for dx in range(1, NX):
        gx_copy(dx, 1).start()

    for s in range(2):
        for dx in range(1, NX):
            wx_copy(dx, s).wait_recv()
    hidden = dot(gbuf[...], wfull[...])
    for h in range(ND):
        for e in range(NE):
            i = h * NE + e
            hsend[h, e] = hidden[i * CAP : (i + 1) * CAP]

    def hb_copy(de, dh):
        e_to = lax.rem(exp + de, NE)
        h_to = lax.rem(core + dh, ND)
        i = de * ND + dh
        return remote(
            hsend.at[h_to, e_to], hrecv.at[core, exp], hb_s.at[i], hb_r.at[i], (ctx, e_to, h_to)
        )

    for de in range(NE):
        for dh in range(ND):
            if de == 0 and dh == 0:
                hrecv[core, exp] = hsend[core, exp]
            else:
                hb_copy(de, dh).start()

    for h in range(GROUP):
        dq_out[:, h * HD : (h + 1) * HD] = (
            jnp.transpose(dq_acc[:, h * QRY : (h + 1) * QRY]) * inv_root
        ).astype(BF16)

    def dz_copy(dz):
        return remote(
            dkv_zs.at[zpeer(dz)],
            dkv_zr.at[dz - 1],
            dz_s.at[dz - 1],
            dz_r.at[dz - 1],
            (zpeer(dz) * NX + x, exp, core),
        )

    for dx in range(1, NX):
        dx_copy(dx).wait_recv()

    @pl.loop(0, NZ)
    def _(zz):
        sums = dkv[x, zz].astype(F32)
        for i in range(NX - 1):
            sums = sums + dkv_x[i, zz].astype(F32)
        dkv_zs[zz] = sums.astype(BF16)

    for dz in range(1, NZ):
        dz_copy(dz).start()

    def gz_copy(dz, s, h):
        return remote(
            wg_zs.at[s, h],
            wg_zr.at[z],
            gz_s.at[s * 2 + h],
            gz_r.at[z],
            ((2 * core + s) * NX + x, exp, h),
        )

    wg_zs[:, :, WS:WP] = jnp.zeros((2, ND, WP - WS, FF), BF16)
    for s in range(2):
        for dx in range(1, NX):
            gx_copy(dx, s).wait_recv()
        sums = wg[pl.ds(pl.multiple_of((s * NX + x) * WB, WB), WB)].astype(F32)
        for i in range(NX - 1):
            sums = sums + wg_x[i, s].astype(F32)
        for h in range(ND):
            wg_zs[s, h, 0:WS] = sums[h * WS : (h + 1) * WS].astype(BF16)
            own = (2 * core + s == z) & (core == h)

            @pl.when(own)
            def _():
                wg_zr[z] = wg_zs[s, h]

            @pl.when(jnp.logical_not(own))
            def _():
                gz_copy(0, s, h).start()

    for de in range(NE):
        for dh in range(ND):
            if de or dh:
                hb_copy(de, dh).wait_recv()
    back = jnp.concatenate([hrecv[0, e] + hrecv[1, e] for e in range(NE)], axis=0)
    high = back.astype(BF16)
    low = (back - high.astype(F32)).astype(BF16)
    mine = dot(perm[...], high, TN) + dot(perm[...], low, TN)
    hid_out[...] = (prob_ref[...] * mine).astype(BF16)
    route_out[...] = jnp.sum(act_ref[...].astype(F32) * mine, axis=1, keepdims=True).astype(BF16)

    for dz in range(1, NZ):
        dz_copy(dz).wait_recv()
    sums = dkv_zs[z].astype(F32)
    for i in range(NZ - 1):
        sums = sums + dkv_zr[i].astype(F32)
    dk_out[...] = sums[0:KEYS].astype(BF16)
    dv_out[...] = sums[KEYS:].astype(BF16)

    for zz in range(NZ):

        @pl.when(jnp.logical_not((zz == z) & (core == w_core)))
        def _():
            remote(
                wg_zs.at[0, 0], wg_zr.at[zz], gz_s.at[0], gz_r.at[zz], (ctx, exp, core)
            ).wait_recv()

    sums = wg_zr[0].astype(F32)
    for zz in range(1, NZ):
        sums = sums + wg_zr[zz].astype(F32)
    dw_out[...] = sums[0:WS].astype(BF16)

    for dz in range(1, NZ):
        kz_copy(dz).wait_send()
        wz_copy(dz).wait_send()
        dz_copy(dz).wait_send()

    @pl.when(jnp.logical_not(w_here))
    def _():
        wz_copy(0).wait_send()

    for dx in range(1, NX):
        for dz in range(NZ):
            kx_copy(dx, dz).wait_send()
        for s in range(2):
            wx_copy(dx, s).wait_send()
            gx_copy(dx, s).wait_send()
        dx_copy(dx).wait_send()
    for de in range(NE):
        for dh in range(ND):
            if de or dh:
                tk_copy(de, dh).wait_send()
                hb_copy(de, dh).wait_send()
    for s in range(2):
        for h in range(ND):

            @pl.when(jnp.logical_not((2 * core + s == z) & (core == h)))
            def _():
                gz_copy(0, s, h).wait_send()


def per_device(
    query,
    key_rows,
    value_rows,
    out_grad,
    block_offsets,
    tok_grad,
    hidden_act,
    router_prob,
    expert_ids,
    down_weight,
):
    vmem = pl.BlockSpec(memory_space=pltpu.VMEM)
    smem = pl.BlockSpec(memory_space=pltpu.SMEM)
    dma = pltpu.SemaphoreType.DMA
    scratch = [
        pltpu.VMEM((NX, NZ, 2 * KEYS, HD), BF16),
        pltpu.VMEM((COLS, HD), BF16),
        pltpu.VMEM((COLS, HD), BF16),
        pltpu.VMEM((1, COLS), F32),
        pltpu.VMEM((1, COLS), F32),
        pltpu.VMEM((1, COLS), F32),
        pltpu.VMEM((KEYS, COLS), BF16),
        pltpu.VMEM((KEYS, COLS), BF16),
        pltpu.VMEM((HD, COLS), F32),
        pltpu.VMEM((NX, NZ, 2 * KEYS, HD), BF16),
        pltpu.VMEM((NX - 1, NZ, 2 * KEYS, HD), BF16),
        pltpu.VMEM((NZ, 2 * KEYS, HD), BF16),
        pltpu.VMEM((NZ - 1, 2 * KEYS, HD), BF16),
        pltpu.VMEM((SLOTS, TOK), BF16),
        pltpu.VMEM((ND, NE, 2 * CAP, PART), BF16),
        pltpu.VMEM((ND, NE, 2 * CAP, PART), BF16),
        pltpu.VMEM((ROWS, HALF), BF16),
        pltpu.VMEM((ROWS, FF), BF16),
        pltpu.VMEM((WP, FF), BF16),
        pltpu.VMEM((2, ND, WP, FF), BF16),
        pltpu.VMEM((HALF, FF), BF16),
        pltpu.VMEM((HALF, FF), BF16),
        pltpu.VMEM((NX - 1, 2, WB, FF), BF16),
        pltpu.VMEM((2, ND, WP, FF), BF16),
        pltpu.VMEM((NZ, WP, FF), BF16),
        pltpu.VMEM((ND, NE, CAP, FF), F32),
        pltpu.VMEM((ND, NE, CAP, FF), F32),
        dma((NZ - 1,)),
        dma((NZ - 1,)),
        dma(((NX - 1) * NZ,)),
        dma(((NX - 1) * NZ,)),
        dma((NZ,)),
        dma((2 * ND,)),
        dma(((NX - 1) * 2,)),
        dma(((NX - 1) * 2,)),
        dma((NE * ND,)),
        dma((NE * ND,)),
        dma((NX - 1,)),
        dma((NX - 1,)),
        dma((NZ - 1,)),
        dma((NZ - 1,)),
        dma(((NX - 1) * 2,)),
        dma(((NX - 1) * 2,)),
        dma((2 * ND,)),
        dma((NZ,)),
        dma((NE * ND,)),
        dma((NE * ND,)),
    ]
    dq, dk, dv, hidden, route, dw = pl.pallas_call(
        kernel,
        name="layer_backward",
        out_shape=(
            jax.ShapeDtypeStruct((QRY, GROUP * HD), BF16),
            jax.ShapeDtypeStruct((KEYS, HD), BF16),
            jax.ShapeDtypeStruct((KEYS, HD), BF16),
            jax.ShapeDtypeStruct((TOK, FF), BF16),
            jax.ShapeDtypeStruct((TOK, 1), BF16),
            jax.ShapeDtypeStruct((WS, FF), BF16),
        ),
        in_specs=[smem] + [vmem] * 10,
        out_specs=[vmem] * 6,
        scratch_shapes=scratch,
        compiler_params=pltpu.CompilerParams(
            collective_id=0, has_side_effects=True, vmem_limit_bytes=60 << 20
        ),
    )(
        block_offsets,
        query[0],
        key_rows[0],
        value_rows[0],
        out_grad[0],
        tok_grad,
        hidden_act,
        router_prob.astype(F32)[:, None],
        expert_ids.reshape(1, TOK),
        expert_ids,
        down_weight[0],
    )
    return (dq[None], dk[None], dv[None], hidden, route[:, 0], dw[None])


def solution(mesh):
    in_specs = (
        P("dp", "ctx", "exp"),
        P("dp", "ctx", "exp"),
        P("dp", "ctx", "exp"),
        P("dp", "ctx", "exp"),
        P(),
        P(("ctx", "exp", "dp"), None),
        P(("ctx", "exp", "dp"), None),
        P(("ctx", "exp", "dp")),
        P(("ctx", "exp", "dp"), None),
        P("exp", ("ctx", "dp"), None),
    )
    out_specs = (
        P("dp", "ctx", "exp"),
        P("dp", "ctx", "exp"),
        P("dp", "ctx", "exp"),
        P(("ctx", "exp", "dp"), None),
        P(("ctx", "exp", "dp")),
        P("exp", ("ctx", "dp"), None),
    )
    return jax.shard_map(
        per_device, mesh=mesh, in_specs=in_specs, out_specs=out_specs, check_vma=False
    )
```

time: 589 us -> 185 us (0.31)
  waiting for transfers between devices: 355 us -> 0 us
  Pallas kernels: 0 us -> 171 us
  matrix products: 135 us -> 0 us
  starting transfers between devices: 26.7 us -> 0 us
  local copies, waits for them, and re-layouts: 33 us -> 10.1 us
  other arithmetic: 18.2 us -> 2.04 us
  between operations: 14.9 us -> 0.64 us
    pallas_call x0 -> x1, Pallas kernels: none -> 171 us  [per_device(): pl.pallas_call(kernel, name='layer_backward', out_shape=(jax.ShapeDtypeSt...]
    unnamed x7 -> x0, waiting for transfers between devices: 143 us -> none
    dot_general x59 -> x0, matrix products: 135 us -> none  [the longest x8 28.2 us: first_step(): jnp.einsum('hqk,kd->hqd', unnormed, value_block.astype(jnp.float32), prec...]
    reduce_scatter x2 -> x0, waiting for transfers between devices: 131 us -> none  [the longest x1 88.3 us: per_device(): lax.psum_scatter(value_acc.astype(jnp.bfloat16), 'ctx', scatter_dimension...]
    all_gather x3 -> x0, waiting for transfers between devices: 79.4 us -> none  [the longest x1 53.2 us: per_device(): lax.all_gather(value_rows[0], 'ctx', axis=0, tiled=True)]
    all_to_all x5 -> x0, starting transfers between devices: 26.6 us -> none  [the longest x1 5.6 us: per_device(): lax.all_to_all(send_prob, 'exp', split_axis=0, concat_axis=0, tiled=True)]
    while x42 -> x0, local copies, waits for them, and re-layouts: 11.9 us -> none
    scatter x3 -> x0, local copies, waits for them, and re-layouts: 9.1 us -> none  [the longest x1 5.47 us: per_device(): send_grad = jnp.zeros((slot_total, model_width), jnp.bfloat16).at[target]...]
  transfers between devices with their start and end apart: 11 -> 0, of which waited for: 6 -> 0; matrix products, arithmetic and copies ran while one was open for 30% -> 0% of each run, Pallas kernels for 0% -> 0%
where the time goes in v1:
time: 185 us; the launch traced here: 184 us
  Pallas kernels  171 us (92%)
  local copies, waits for them, and re-layouts  10.1 us (5%)
  other arithmetic  2.04 us (1%)
    pallas_call x1, Pallas kernels, per_device(): pl.pallas_call(kernel, name='layer_backward', out_shape=(jax.ShapeDtypeSt...  171 us
    unnamed x6, local copies, waits for them, and re-layouts  9.31 us

profile of v1, /device:TPU:81, one launch (start us, length us, event | category | flops | bytes accessed | tf_op | source)
XLA Modules:
  0.0 184.1 jit_solution(3827996701972365057)
XLA Ops:
  0.6 0.7 bitcast_convert_fusion
  1.3 0.7 copy.18.prob_ref
  2.0 1.4 copy.19.idc_ref
  3.4 171.4 %layer_backward.1 = (bf16[128,1280]{1,0:T(8,128)(2,1)}, bf16[256,128]{1,0:T(8,128)(2,1)}, bf16[256,128]{1,0:T(8,128)(2,1)}, bf16[128,640]{1,0:T(8,128)(2,1)}, bf...) custom-call(s32[16]{0:T(128)} %off_ref.1, bf16[128,1280]{1,0:T(8,128)(2,1)} %bitcast.13, bf16[256,128]{1,0:T(8,128)(2,1)} %bitcast.18, ...), custom_call_target="tpu_custom_call" | custom-call | tf_op jit(solution)/shard_map/layer_backward/pallas_call | solution.py:610
  174.8 1.4 reduce
  176.2 1.7 copy.25
  177.9 1.5 copy.26
  179.4 1.5 copy.27
  180.8 1.6 copy.28
  182.4 1.7 copy.29

commit v2 on v1

v2 whole, which is shorter than its diff:
```python
import math

import jax
import jax.numpy as jnp
from jax import lax
from jax.experimental import pallas as pl
from jax.experimental.pallas import tpu as pltpu
from jax.sharding import PartitionSpec as P

HD = 128
GROUP = 10
NEG_FILL = -1e30
MESH = pl.DeviceIdType.MESH
F32 = jnp.float32
BF16 = jnp.bfloat16

NX, NZ, NE, ND = 4, 4, 8, 2
KEYS = 256
QRY = 128
COLS = GROUP * QRY
TOK = 128
CAP = 24
D = 6400
HALF = D // 2
FF = 640
PART = (HALF + FF) // 2
WB = 400
WS = 200
WP = 208
SLOTS = NE * CAP
ROWS = ND * SLOTS

NT = (((1,), (1,)), ((), ()))
TN = (((0,), (0,)), ((), ()))


def dot(a, b, dims=(((1,), (0,)), ((), ()))):
    return lax.dot_general(a, b, dims, preferred_element_type=F32)


def kernel(
    off_ref,
    q_ref,
    k_ref,
    v_ref,
    do_ref,
    tok_ref,
    act_ref,
    prob_ref,
    ids_ref,
    w_ref,
    dq_out,
    dk_out,
    dv_out,
    hid_out,
    route_out,
    dw_out,
    kv,
    qs,
    dos,
    stat_m,
    stat_l,
    stat_d,
    p_buf,
    ds_buf,
    dq_acc,
    dkv,
    dkv_o,
    dkv_n,
    dkv_zs,
    dkv_zr,
    perm,
    tsend,
    trecv,
    gbuf,
    abuf,
    wpad,
    wraw,
    wfull,
    wg,
    wg_oa,
    wg_ob,
    wg_n,
    wg_zs,
    wg_zr,
    hsend,
    hrecv,
    kz_s,
    kz_r,
    kx_s,
    kx_r,
    kf_s,
    kf_r,
    wz_s,
    wz_r,
    wx_s,
    wx_r,
    wf_s,
    wf_r,
    tk_s,
    tk_r,
    do_s,
    do_r,
    dn_s,
    dn_r,
    dz_s,
    dz_r,
    go_s,
    go_r,
    gn_s,
    gn_r,
    gz_s,
    gz_r,
    hb_s,
    hb_r,
):
    ctx = lax.axis_index("ctx")
    exp = lax.axis_index("exp")
    core = lax.axis_index("dp")
    z = ctx // NX
    x = ctx % NX
    inv_root = 1.0 / math.sqrt(HD)
    scale2 = inv_root * math.log2(math.e)

    def xpeer(dx):
        return lax.rem(x + dx, NX)

    def zpeer(dz):
        return lax.rem(z + dz, NZ)

    def remote(src, dst, ss, rs, dev):
        return pltpu.make_async_remote_copy(
            src_ref=src, dst_ref=dst, send_sem=ss, recv_sem=rs, device_id=dev, device_id_type=MESH
        )

    step = (1, NX - 1)
    back = (NX - 1, 1)
    near = tuple((z * NX + xpeer(d), exp, core) for d in step)
    sent = []

    def go(copy):
        copy.start()
        sent.append(copy)

    partners = list(near)
    for dz in range(0, NZ):
        for dh in range(ND):
            if dz or dh:
                partners.append((zpeer(dz) * NX + x, exp, lax.rem(core + dh, ND)))
    for de in range(1, NE):
        for dh in range(ND):
            partners.append((ctx, lax.rem(exp + de, NE), lax.rem(core + dh, ND)))
    barrier = pltpu.get_barrier_semaphore()
    for partner in partners:
        pl.semaphore_signal(barrier, inc=1, device_id=partner, device_id_type=MESH)
    pl.semaphore_wait(barrier, len(partners))

    kv[x, z, 0:KEYS] = k_ref[...]
    kv[x, z, KEYS : 2 * KEYS] = v_ref[...]
    halves = (pl.ds(0, KEYS), pl.ds(KEYS, KEYS))

    def kz_copy(dz):
        return remote(
            kv.at[x, z],
            kv.at[x, z],
            kz_s.at[dz - 1],
            kz_r.at[dz - 1],
            (zpeer(dz) * NX + x, exp, core),
        )

    def kx_copy(way, dz, xx):
        at = kv.at[xx, zpeer(NZ - dz)]
        return remote(at, at, kx_s.at[way * NZ + dz], kx_r.at[way * NZ + dz], near[way])

    def kf_copy(way, dz, xx):
        at = kv.at[xx, zpeer(NZ - dz), halves[way]]
        return remote(at, at, kf_s.at[way * NZ + dz], kf_r.at[way * NZ + dz], near[way])

    for dz in (1, 3, 2):
        go(kz_copy(dz))
    for way in range(2):
        go(kx_copy(way, 0, x))

    wpad[0:WS] = w_ref[...]
    wpad[WS:WP] = jnp.zeros((WP - WS, FF), BF16)
    w_core = z // 2
    w_slot = lax.rem(z, 2)
    w_here = core == w_core

    def wz_copy(dz):
        return remote(
            wpad,
            wraw.at[w_slot, core],
            wz_s.at[dz],
            wz_r.at[w_slot * 2 + core],
            (zpeer(dz) * NX + x, exp, w_core),
        )

    for dz in (1, 3, 2):
        go(wz_copy(dz))

    @pl.when(w_here)
    def _():
        wraw[w_slot, core] = wpad[...]

    @pl.when(jnp.logical_not(w_here))
    def _():
        wz_copy(0).start()

    row_at = lax.broadcasted_iota(jnp.int32, (TOK, TOK), 0)
    col_at = lax.broadcasted_iota(jnp.int32, (TOK, TOK), 1)
    eye = row_at == col_at

    def column(row):
        return jnp.sum(jnp.where(eye, row, 0.0), axis=1, keepdims=True)

    ids_row = ids_ref[...]
    ids_f = ids_row.astype(F32)
    prob_col = column(prob_ref[...].astype(F32))
    same = jnp.where((column(ids_f) == ids_f) & (row_at < col_at), 1.0, 0.0)
    rank = jnp.sum(same, axis=0, keepdims=True).astype(jnp.int32)
    target = ids_row * CAP + rank
    slot_at = lax.broadcasted_iota(jnp.int32, (SLOTS, TOK), 0)
    perm[...] = jnp.where(slot_at == target, 1.0, 0.0).astype(BF16)
    scaled_act = (prob_col * act_ref[...].astype(F32)).astype(BF16)

    def tk_copy(de, dh):
        e_to = lax.rem(exp + de, NE)
        h_to = lax.rem(core + dh, ND)
        i = de * ND + dh
        return remote(
            tsend.at[h_to, e_to],
            trecv.at[core, exp],
            tk_s.at[i],
            tk_r.at[i],
            (ctx, e_to, h_to),
        )

    for half in range(ND):
        base = half * HALF
        first = dot(perm[...], tok_ref[:, base : base + PART])
        second = dot(perm[...], tok_ref[:, base + PART : base + HALF])
        third = dot(perm[...], scaled_act)
        for e in range(NE):
            rows = slice(e * CAP, (e + 1) * CAP)
            tsend[half, e, :, 0 : HALF - PART] = jnp.concatenate(
                [first[rows, 0 : HALF - PART], second[rows]], axis=0
            ).astype(BF16)
            tsend[half, e, :, HALF - PART : PART] = jnp.concatenate(
                [first[rows, HALF - PART : PART], third[rows]], axis=0
            ).astype(BF16)
    trecv[core, exp] = tsend[core, exp]
    go(tk_copy(0, 1))
    for de in (4, 2, 6):
        for dh in range(ND):
            go(tk_copy(de, dh))

    for dz in (1, 3, 2):
        kz_copy(dz).wait_recv()
        for way in range(2):
            go(kx_copy(way, dz, x))

    w_halves = ((0, WP), (WP, WB - WP))

    def w_rows(xx, s, part=None):
        start = (s * NX + xx) * WB
        if part is None:
            return pl.ds(pl.multiple_of(start, 16), WB)
        return pl.ds(pl.multiple_of(start + w_halves[part][0], 16), w_halves[part][1])

    def wx_copy(way, s, xx):
        at = wfull.at[w_rows(xx, s)]
        return remote(at, at, wx_s.at[way * 2 + s], wx_r.at[way * 2 + s], near[way])

    def wf_copy(way, s, xx):
        at = wfull.at[w_rows(xx, s, way)]
        return remote(at, at, wf_s.at[way * 2 + s], wf_r.at[way * 2 + s], near[way])

    for s in range(2):
        for h in range(ND):

            @pl.when(jnp.logical_not((2 * core + s == z) & (core == h)))
            def _():
                remote(
                    wpad, wraw.at[s, h], wz_s.at[0], wz_r.at[s * 2 + h], (ctx, exp, core)
                ).wait_recv()

        merged = jnp.concatenate(
            [wraw[s, 0, 0:WS].astype(F32), wraw[s, 1, 0:WS].astype(F32)], axis=0
        )
        wfull[w_rows(x, s)] = merged.astype(BF16)
        for way in range(2):
            go(wx_copy(way, s, x))

    for de in (1, 7, 3, 5):
        for dh in range(ND):
            go(tk_copy(de, dh))

    for h in range(GROUP):
        qs[h * QRY : (h + 1) * QRY] = q_ref[:, h * HD : (h + 1) * HD]
        dos[h * QRY : (h + 1) * QRY] = do_ref[:, h * HD : (h + 1) * HD]

    for dz in (0, 1, 3, 2):
        for way in range(2):
            xx = xpeer(back[way])
            kx_copy(way, dz, xx).wait_recv()
            go(kf_copy(way, dz, xx))

    own_pos = off_ref[ctx] * KEYS + (KEYS - QRY)
    q_pos = own_pos + lax.broadcasted_iota(jnp.int32, (KEYS, QRY), 1)
    k_at = lax.broadcasted_iota(jnp.int32, (KEYS, QRY), 0)
    wide = 2 * QRY

    def bias_of(xx, zz):
        seen = off_ref[zz * NX + xx] * KEYS + k_at <= q_pos
        one = jnp.where(seen, 0.0, NEG_FILL)
        return jnp.concatenate([one, one], axis=1)

    stat_m[...] = jnp.full((1, COLS), NEG_FILL, F32)
    stat_l[...] = jnp.zeros((1, COLS), F32)
    stat_d[...] = jnp.zeros((1, COLS), F32)

    def first_pass(xx, zz):
        bias = bias_of(xx, zz)
        keys = kv[xx, zz, 0:KEYS]
        values = kv[xx, zz, KEYS : 2 * KEYS]
        for g in range(COLS // wide):
            at = slice(g * wide, (g + 1) * wide)
            scores = dot(keys, qs[at], NT) * scale2 + bias
            grads = dot(values, dos[at], NT)
            old = stat_m[:, at]
            peak = jnp.maximum(old, jnp.max(scores, axis=0, keepdims=True))
            shrink = jnp.exp2(old - peak)
            probs = jnp.exp2(scores - peak)
            stat_m[:, at] = peak
            stat_l[:, at] = stat_l[:, at] * shrink + jnp.sum(probs, axis=0, keepdims=True)
            stat_d[:, at] = stat_d[:, at] * shrink + jnp.sum(probs * grads, axis=0, keepdims=True)

    def forward_weights(s):
        for way in range(2):
            xx = xpeer(back[way])
            wx_copy(way, s, xx).wait_recv()
            go(wf_copy(way, s, xx))

    for dx in (0, 1, 3, 2):
        xx = xpeer(dx)
        if dx == 2:
            for dz in range(NZ):
                for way in range(2):
                    kf_copy(way, dz, xx).wait_recv()

        @pl.loop(0, NZ)
        def _(zz):
            first_pass(xx, zz)

    total = stat_l[...]
    stat_m[...] = stat_m[...] + jnp.log2(total)
    stat_d[...] = stat_d[...] / total
    dq_acc[...] = jnp.zeros((HD, COLS), F32)

    def second_pass(xx, zz):
        bias = bias_of(xx, zz)
        keys = kv[xx, zz, 0:KEYS]
        values = kv[xx, zz, KEYS : 2 * KEYS]
        for g in range(COLS // wide):
            at = slice(g * wide, (g + 1) * wide)
            scores = dot(keys, qs[at], NT) * scale2 + bias
            grads = dot(values, dos[at], NT)
            probs = jnp.exp2(scores - stat_m[:, at])
            p_buf[:, at] = probs.astype(BF16)
            ds_buf[:, at] = (probs * (grads - stat_d[:, at])).astype(BF16)
        dkv[xx, 0, zz] = (dot(ds_buf[...], qs[...]) * inv_root).astype(BF16)
        dkv[xx, 1, zz] = dot(p_buf[...], dos[...]).astype(BF16)
        dq_acc[...] += dot(keys, ds_buf[...], TN)

    def do_copy(way):
        return remote(
            dkv.at[xpeer(2), way], dkv_o.at[way], do_s.at[way], do_r.at[way], near[way]
        )

    def dn_copy(way, part):
        i = way * 2 + part
        return remote(
            dkv.at[xpeer(step[way]), part],
            dkv_n.at[way, part],
            dn_s.at[i],
            dn_r.at[i],
            near[way],
        )

    for dx in (2, 1, 3, 0):
        xx = xpeer(dx)

        @pl.loop(0, NZ)
        def _(zz):
            second_pass(xx, zz)

        if dx == 2:
            for way in range(2):
                go(do_copy(way))
            forward_weights(0)
        elif dx:
            way = step.index(dx)
            go(dn_copy(way, 1 - way))
    forward_weights(1)
    for way in range(2):
        do_copy(way).wait_recv()
        xx = xpeer(step[way])
        dkv[xx, way] = (dkv[xx, way].astype(F32) + dkv_o[way].astype(F32)).astype(BF16)
        go(dn_copy(way, way))

    for de in range(NE):
        for dh in range(ND):
            if de or dh:
                tk_copy(de, dh).wait_recv()

    @pl.loop(0, NE)
    def _(i):
        h = i // (NE // 2)
        e = lax.rem(i, NE // 2) * 2
        one = trecv[h, e].astype(F32)
        two = trecv[h, e + 1].astype(F32)
        at = pl.ds(pl.multiple_of(i * 2 * CAP, 2 * CAP), 2 * CAP)
        gbuf[at, 0:PART] = jnp.concatenate([one[0:CAP], two[0:CAP]], axis=0).astype(BF16)
        rest = jnp.concatenate([one[CAP:], two[CAP:]], axis=0).astype(BF16)
        gbuf[at, PART:HALF] = rest[:, 0 : HALF - PART]
        abuf[at] = rest[:, HALF - PART :]

    def go_copy(way, s):
        return remote(
            wg.at[w_rows(xpeer(2), s, way)],
            (wg_oa, wg_ob)[way].at[s],
            go_s.at[way * 2 + s],
            go_r.at[way * 2 + s],
            near[way],
        )

    def gn_copy(way, s, part):
        i = (way * 2 + s) * 2 + part
        return remote(
            wg.at[w_rows(xpeer(step[way]), s, part)],
            wg_n.at[way, s, pl.ds(w_halves[part][0], w_halves[part][1])],
            gn_s.at[i],
            gn_r.at[i],
            near[way],
        )

    def send_grads(s):
        for way in range(2):
            go(go_copy(way, s))
        for way in range(2):
            go(gn_copy(way, s, 1 - way))

    def join_grads(s):
        for way in range(2):
            go_copy(way, s).wait_recv()
            at = w_rows(xpeer(step[way]), s, way)
            theirs = (wg_oa, wg_ob)[way][s]
            wg[at] = (wg[at].astype(F32) + theirs.astype(F32)).astype(BF16)
            go(gn_copy(way, s, way))

    for i in range(HALF // FF):
        at = slice(i * FF, (i + 1) * FF)
        wg[at] = dot(gbuf[:, at], abuf[...], TN).astype(BF16)
        if i == 2:
            send_grads(0)
    send_grads(1)
    join_grads(0)

    for s in range(2):
        for way in range(2):
            wf_copy(way, s, xpeer(2)).wait_recv()
    hidden = dot(gbuf[...], wfull[...])
    for h in range(ND):
        for e in range(NE):
            i = h * NE + e
            hsend[h, e] = hidden[i * CAP : (i + 1) * CAP]

    def hb_copy(de, dh):
        e_to = lax.rem(exp + de, NE)
        h_to = lax.rem(core + dh, ND)
        i = de * ND + dh
        return remote(
            hsend.at[h_to, e_to], hrecv.at[core, exp], hb_s.at[i], hb_r.at[i], (ctx, e_to, h_to)
        )

    for de in range(NE):
        for dh in range(ND):
            if de == 0 and dh == 0:
                hrecv[core, exp] = hsend[core, exp]
            else:
                go(hb_copy(de, dh))
    join_grads(1)

    def dz_copy(dz):
        return remote(
            dkv_zs.at[zpeer(dz)],
            dkv_zr.at[dz - 1],
            dz_s.at[dz - 1],
            dz_r.at[dz - 1],
            (zpeer(dz) * NX + x, exp, core),
        )

    for way in range(2):
        for part in range(2):
            dn_copy(way, part).wait_recv()

    @pl.loop(0, NZ)
    def _(zz):
        for part in range(2):
            sums = dkv[x, part, zz].astype(F32)
            for way in range(2):
                sums = sums + dkv_n[way, part, zz].astype(F32)
            dkv_zs[zz, part] = sums.astype(BF16)

    for dz in (2, 1, 3):
        go(dz_copy(dz))
    for h in range(GROUP):
        dq_out[:, h * HD : (h + 1) * HD] = (
            jnp.transpose(dq_acc[:, h * QRY : (h + 1) * QRY]) * inv_root
        ).astype(BF16)

    def gz_copy(s, h):
        return remote(
            wg_zs.at[s, h],
            wg_zr.at[z],
            gz_s.at[s * 2 + h],
            gz_r.at[z],
            ((2 * core + s) * NX + x, exp, h),
        )

    def sum_grads(s):
        for way in range(2):
            for part in range(2):
                gn_copy(way, s, part).wait_recv()
        sums = wg[w_rows(x, s)].astype(F32)
        for way in range(2):
            sums = sums + wg_n[way, s].astype(F32)
        for h in range(ND):
            wg_zs[s, h, 0:WS] = sums[h * WS : (h + 1) * WS].astype(BF16)
            own = (2 * core + s == z) & (core == h)

            @pl.when(own)
            def _():
                wg_zr[z] = wg_zs[s, h]

            @pl.when(jnp.logical_not(own))
            def _():
                gz_copy(s, h).start()

    wg_zs[:, :, WS:WP] = jnp.zeros((2, ND, WP - WS, FF), BF16)
    sum_grads(0)

    for de in range(NE):
        for dh in range(ND):
            if de or dh:
                hb_copy(de, dh).wait_recv()
    back_rows = jnp.concatenate([hrecv[0, e] + hrecv[1, e] for e in range(NE)], axis=0)
    high = back_rows.astype(BF16)
    low = (back_rows - high.astype(F32)).astype(BF16)
    mine = dot(perm[...], high, TN) + dot(perm[...], low, TN)
    hid_out[...] = (prob_col * mine).astype(BF16)
    route = jnp.sum(act_ref[...].astype(F32) * mine, axis=1, keepdims=True)
    route_out[...] = jnp.sum(jnp.where(eye, route, 0.0), axis=0, keepdims=True).astype(BF16)

    for dz in range(1, NZ):
        dz_copy(dz).wait_recv()
    for part, out in enumerate((dk_out, dv_out)):
        sums = dkv_zs[z, part].astype(F32)
        for i in range(NZ - 1):
            sums = sums + dkv_zr[i, part].astype(F32)
        out[...] = sums.astype(BF16)

    sum_grads(1)
    for zz in range(NZ):

        @pl.when(jnp.logical_not((zz == z) & (core == w_core)))
        def _():
            remote(
                wg_zs.at[0, 0], wg_zr.at[zz], gz_s.at[0], gz_r.at[zz], (ctx, exp, core)
            ).wait_recv()

    sums = wg_zr[0].astype(F32)
    for zz in range(1, NZ):
        sums = sums + wg_zr[zz].astype(F32)
    dw_out[...] = sums[0:WS].astype(BF16)

    for copy in sent:
        copy.wait_send()

    @pl.when(jnp.logical_not(w_here))
    def _():
        wz_copy(0).wait_send()

    for s in range(2):
        for h in range(ND):

            @pl.when(jnp.logical_not((2 * core + s == z) & (core == h)))
            def _():
                gz_copy(s, h).wait_send()


def finish(*refs):
    count = len(refs) // 2
    for source, out in zip(refs[:count], refs[count:]):
        out[...] = source[...]


def per_device(
    query,
    key_rows,
    value_rows,
    out_grad,
    block_offsets,
    tok_grad,
    hidden_act,
    router_prob,
    expert_ids,
    down_weight,
):
    vmem = pl.BlockSpec(memory_space=pltpu.VMEM)
    smem = pl.BlockSpec(memory_space=pltpu.SMEM)
    dma = pltpu.SemaphoreType.DMA
    scratch = [
        pltpu.VMEM((NX, NZ, 2 * KEYS, HD), BF16),
        pltpu.VMEM((COLS, HD), BF16),
        pltpu.VMEM((COLS, HD), BF16),
        pltpu.VMEM((1, COLS), F32),
        pltpu.VMEM((1, COLS), F32),
        pltpu.VMEM((1, COLS), F32),
        pltpu.VMEM((KEYS, COLS), BF16),
        pltpu.VMEM((KEYS, COLS), BF16),
        pltpu.VMEM((HD, COLS), F32),
        pltpu.VMEM((NX, 2, NZ, KEYS, HD), BF16),
        pltpu.VMEM((2, NZ, KEYS, HD), BF16),
        pltpu.VMEM((2, 2, NZ, KEYS, HD), BF16),
        pltpu.VMEM((NZ, 2, KEYS, HD), BF16),
        pltpu.VMEM((NZ - 1, 2, KEYS, HD), BF16),
        pltpu.VMEM((SLOTS, TOK), BF16),
        pltpu.VMEM((ND, NE, 2 * CAP, PART), BF16),
        pltpu.VMEM((ND, NE, 2 * CAP, PART), BF16),
        pltpu.VMEM((ROWS, HALF), BF16),
        pltpu.VMEM((ROWS, FF), BF16),
        pltpu.VMEM((WP, FF), BF16),
        pltpu.VMEM((2, ND, WP, FF), BF16),
        pltpu.VMEM((HALF, FF), BF16),
        pltpu.VMEM((HALF, FF), BF16),
        pltpu.VMEM((2, WP, FF), BF16),
        pltpu.VMEM((2, WB - WP, FF), BF16),
        pltpu.VMEM((2, 2, WB, FF), BF16),
        pltpu.VMEM((2, ND, WP, FF), BF16),
        pltpu.VMEM((NZ, WP, FF), BF16),
        pltpu.VMEM((ND, NE, CAP, FF), F32),
        pltpu.VMEM((ND, NE, CAP, FF), F32),
    ]
    for size in (
        NZ - 1,
        2 * NZ,
        2 * NZ,
        NZ,
        4,
        4,
        NE * ND,
        2,
        4,
        NZ - 1,
        4,
        8,
        NZ,
        NE * ND,
    ):
        scratch += [dma((size,)), dma((size,))]
    shapes = (
        jax.ShapeDtypeStruct((QRY, GROUP * HD), BF16),
        jax.ShapeDtypeStruct((KEYS, HD), BF16),
        jax.ShapeDtypeStruct((KEYS, HD), BF16),
        jax.ShapeDtypeStruct((TOK, FF), BF16),
        jax.ShapeDtypeStruct((1, TOK), BF16),
        jax.ShapeDtypeStruct((WS, FF), BF16),
    )
    results = pl.pallas_call(
        kernel,
        name="layer_backward",
        out_shape=shapes,
        in_specs=[smem] + [vmem] * 9,
        out_specs=[vmem] * 6,
        scratch_shapes=scratch,
        compiler_params=pltpu.CompilerParams(
            collective_id=0, has_side_effects=True, vmem_limit_bytes=60 << 20
        ),
    )(
        block_offsets,
        query[0],
        key_rows[0],
        value_rows[0],
        out_grad[0],
        tok_grad,
        hidden_act,
        router_prob.reshape(1, TOK),
        expert_ids.reshape(1, TOK),
        down_weight[0],
    )
    dq, dk, dv, hidden, route, dw = pl.pallas_call(
        finish, name="finish", out_shape=shapes, in_specs=[vmem] * 6, out_specs=[vmem] * 6
    )(*results)
    return (dq[None], dk[None], dv[None], hidden, route[0], dw[None])


def solution(mesh):
    in_specs = (
        P("dp", "ctx", "exp"),
        P("dp", "ctx", "exp"),
        P("dp", "ctx", "exp"),
        P("dp", "ctx", "exp"),
        P(),
        P(("ctx", "exp", "dp"), None),
        P(("ctx", "exp", "dp"), None),
        P(("ctx", "exp", "dp")),
        P(("ctx", "exp", "dp"), None),
        P("exp", ("ctx", "dp"), None),
    )
    out_specs = (
        P("dp", "ctx", "exp"),
        P("dp", "ctx", "exp"),
        P("dp", "ctx", "exp"),
        P(("ctx", "exp", "dp"), None),
        P(("ctx", "exp", "dp")),
        P("exp", ("ctx", "dp"), None),
    )
    return jax.shard_map(
        per_device, mesh=mesh, in_specs=in_specs, out_specs=out_specs, check_vma=False
    )
```

time: 185 us -> 164 us (0.89)
  local copies, waits for them, and re-layouts: 10.1 us -> 0 us
  Pallas kernels: 171 us -> 163 us
  other arithmetic: 2.04 us -> 0 us
    unnamed x6 -> x0, local copies, waits for them, and re-layouts: 9.31 us -> none
    pallas_call x1 -> x2, Pallas kernels: 171 us -> 163 us  [the longest x1 161 us: per_device(): pl.pallas_call(kernel, name='layer_backward', out_shape=shapes, in_specs=...]
where the time goes in v2:
time: 164 us
  Pallas kernels  163 us (99%)
    pallas_call x1, Pallas kernels, per_device(): pl.pallas_call(kernel, name='layer_backward', out_shape=shapes, in_specs=...  161 us

profile of v2, /device:TPU:81, one launch (start us, length us, event | category | flops | bytes accessed | tf_op | source)
XLA Modules:
  0.0 164.0 jit_solution(11714960121600420638)
XLA Ops:
  0.6 161.3 %layer_backward.1 = (bf16[128,1280]{1,0:T(8,128)(2,1)}, bf16[256,128]{1,0:T(8,128)(2,1)}, bf16[256,128]{1,0:T(8,128)(2,1)}, bf16[128,640]{1,0:T(8,128)(2,1)}, bf...) custom-call(s32[16]{0:T(128)} %off_ref.1, bf16[128,1280]{1,0:T(8,128)(2,1)} %bitcast.12, bf16[256,128]{1,0:T(8,128)(2,1)} %bitcast.15, ...), custom_call_target="tpu_custom_call" | custom-call | tf_op jit(solution)/shard_map/layer_backward/pallas_call | solution.py:681
  161.9 2.1 %finish.1 = (bf16[128,1280]{1,0:T(8,128)(2,1)}, bf16[256,128]{1,0:T(8,128)(2,1)}, bf16[256,128]{1,0:T(8,128)(2,1)}, bf16[128,640]{1,0:T(8,128)(2,1)}, bf16[1,128]{1,0:T(2,128)(2,1)}, /*index=5*/bf16[200,640]{1,0:T(8,128)(2,1)}) custom-call(bf16[128,1280]{1,0:T(8,128)(2,1)} %get-tuple-element.18.refs_0_, bf16[256,128]{1,0:T(8,128)(2,1)} %get-tuple-element.19.refs_1_, ...), custom_call_target="tpu_custom_call" | custom-call | tf_op jit(solution)/shard_map/finish/pallas_call | solution.py:703

commit v3 on v2

--- a/solution.py
+++ b/solution.py
@@ -84,15 +84,21 @@
     wg_zs,
     wg_zr,
     hsend,
+    hother,
+    hsum,
     hrecv,
     kz_s,
     kz_r,
+    kg_s,
+    kg_r,
     kx_s,
     kx_r,
     kf_s,
     kf_r,
     wz_s,
     wz_r,
+    wg_s,
+    wg_r,
     wx_s,
     wx_r,
     wf_s,
@@ -111,6 +117,8 @@
     gn_r,
     gz_s,
     gz_r,
+    hx_s,
+    hx_r,
     hb_s,
     hb_r,
 ):
@@ -159,14 +167,15 @@
     kv[x, z, KEYS : 2 * KEYS] = v_ref[...]
     halves = (pl.ds(0, KEYS), pl.ds(KEYS, KEYS))
 
-    def kz_copy(dz):
-        return remote(
-            kv.at[x, z],
-            kv.at[x, z],
-            kz_s.at[dz - 1],
-            kz_r.at[dz - 1],
-            (zpeer(dz) * NX + x, exp, core),
-        )
+    above = tuple((zpeer(d) * NX + x, exp, core) for d in step)
+
+    def kz_copy(way, zz):
+        at = kv.at[x, zz]
+        return remote(at, at, kz_s.at[way], kz_r.at[way], above[way])
+
+    def kg_copy(way, zz):
+        at = kv.at[x, zz, halves[way]]
+        return remote(at, at, kg_s.at[way], kg_r.at[way], above[way])
 
     def kx_copy(way, dz, xx):
         at = kv.at[xx, zpeer(NZ - dz)]
@@ -176,8 +185,8 @@
         at = kv.at[xx, zpeer(NZ - dz), halves[way]]
         return remote(at, at, kf_s.at[way * NZ + dz], kf_r.at[way * NZ + dz], near[way])
 
-    for dz in (1, 3, 2):
-        go(kz_copy(dz))
+    for way in range(2):
+        go(kz_copy(way, z))
     for way in range(2):
         go(kx_copy(way, 0, x))
 
@@ -196,7 +205,7 @@
             (zpeer(dz) * NX + x, exp, w_core),
         )
 
-    for dz in (1, 3, 2):
+    for dz in step:
         go(wz_copy(dz))
 
     @pl.when(w_here)
@@ -206,6 +215,43 @@
     @pl.when(jnp.logical_not(w_here))
     def _():
         wz_copy(0).start()
+
+    z_halves = (pl.ds(0, 112), pl.ds(112, WP - 112))
+
+    def wz_wait(s, h):
+        remote(wpad, wraw.at[s, h], wz_s.at[0], wz_r.at[s * 2 + h], (ctx, exp, core)).wait_recv()
+
+    def wf_zcopy(way, zz, h):
+        at = wraw.at[lax.rem(zz, 2), h, z_halves[way]]
+        i = way * 2 + h
+        return remote(at, at, wg_s.at[i], wg_r.at[i], above[way])
+
+    w_halves = ((0, WP), (WP, WB - WP))
+
+    def w_rows(xx, s, part=None):
+        start = (s * NX + xx) * WB
+        if part is None:
+            return pl.ds(pl.multiple_of(start, 16), WB)
+        return pl.ds(pl.multiple_of(start + w_halves[part][0], 16), w_halves[part][1])
+
+    def wx_copy(way, s, xx):
+        at = wfull.at[w_rows(xx, s)]
+        return remote(at, at, wx_s.at[way * 2 + s], wx_r.at[way * 2 + s], near[way])
+
+    def wf_copy(way, s, xx):
+        at = wfull.at[w_rows(xx, s, way)]
+        return remote(at, at, wf_s.at[way * 2 + s], wf_r.at[way * 2 + s], near[way])
+
+    def place_weights(s):
+        merged = jnp.concatenate(
+            [wraw[s, 0, 0:WS].astype(F32), wraw[s, 1, 0:WS].astype(F32)], axis=0
+        )
+        wfull[w_rows(x, s)] = merged.astype(BF16)
+        for way in range(2):
+            wx_copy(way, s, x).start()
+
+    w_other = lax.rem(z + 1, 2)
+    w_first = lax.rem(z + (core - w_core) * (core - w_core), 2)
 
     row_at = lax.broadcasted_iota(jnp.int32, (TOK, TOK), 0)
     col_at = lax.broadcasted_iota(jnp.int32, (TOK, TOK), 1)
@@ -249,52 +295,38 @@
             tsend[half, e, :, HALF - PART : PART] = jnp.concatenate(
                 [first[rows, HALF - PART : PART], third[rows]], axis=0
             ).astype(BF16)
+
+    @pl.when(w_here)
+    def _():
+        wz_wait(w_slot, 1 - core)
+        place_weights(w_slot)
+
     trecv[core, exp] = tsend[core, exp]
     go(tk_copy(0, 1))
     for de in (4, 2, 6):
         for dh in range(ND):
             go(tk_copy(de, dh))
 
-    for dz in (1, 3, 2):
-        kz_copy(dz).wait_recv()
-        for way in range(2):
-            go(kx_copy(way, dz, x))
-
-    w_halves = ((0, WP), (WP, WB - WP))
-
-    def w_rows(xx, s, part=None):
-        start = (s * NX + xx) * WB
-        if part is None:
-            return pl.ds(pl.multiple_of(start, 16), WB)
-        return pl.ds(pl.multiple_of(start + w_halves[part][0], 16), w_halves[part][1])
-
-    def wx_copy(way, s, xx):
-        at = wfull.at[w_rows(xx, s)]
-        return remote(at, at, wx_s.at[way * 2 + s], wx_r.at[way * 2 + s], near[way])
-
-    def wf_copy(way, s, xx):
-        at = wfull.at[w_rows(xx, s, way)]
-        return remote(at, at, wf_s.at[way * 2 + s], wf_r.at[way * 2 + s], near[way])
-
-    for s in range(2):
-        for h in range(ND):
-
-            @pl.when(jnp.logical_not((2 * core + s == z) & (core == h)))
-            def _():
-                remote(
-                    wpad, wraw.at[s, h], wz_s.at[0], wz_r.at[s * 2 + h], (ctx, exp, core)
-                ).wait_recv()
-
-        merged = jnp.concatenate(
-            [wraw[s, 0, 0:WS].astype(F32), wraw[s, 1, 0:WS].astype(F32)], axis=0
-        )
-        wfull[w_rows(x, s)] = merged.astype(BF16)
-        for way in range(2):
-            go(wx_copy(way, s, x))
-
-    for de in (1, 7, 3, 5):
-        for dh in range(ND):
-            go(tk_copy(de, dh))
+    for way in range(2):
+        zz = zpeer(back[way])
+        kz_copy(way, zz).wait_recv()
+        go(kg_copy(way, zz))
+        for to in range(2):
+            go(kx_copy(to, back[1 - way], x))
+    for way in range(2):
+        zz = zpeer(back[way])
+
+        @pl.when(core == zz // 2)
+        def _():
+            for h in range(ND):
+                wz_wait(lax.rem(zz, 2), h)
+                wf_zcopy(way, zz, h).start()
+
+    for way in range(2):
+        kg_copy(way, zpeer(2)).wait_recv()
+    for way in range(2):
+        go(kx_copy(way, 2, x))
+    place_weights(w_other)
 
     for h in range(GROUP):
         qs[h * QRY : (h + 1) * QRY] = q_ref[:, h * HD : (h + 1) * HD]
@@ -344,6 +376,17 @@
 
     for dx in (0, 1, 3, 2):
         xx = xpeer(dx)
+        if dx == 1:
+            @pl.when(jnp.logical_not(w_here))
+            def _():
+                for h in range(ND):
+                    for way in range(2):
+                        wf_zcopy(way, zpeer(2), h).wait_recv()
+                place_weights(w_slot)
+
+            for de in (1, 7, 3, 5):
+                for dh in range(ND):
+                    go(tk_copy(de, dh))
         if dx == 2:
             for dz in range(NZ):
                 for way in range(2):
@@ -388,43 +431,26 @@
             near[way],
         )
 
-    for dx in (2, 1, 3, 0):
-        xx = xpeer(dx)
-
-        @pl.loop(0, NZ)
-        def _(zz):
-            second_pass(xx, zz)
-
-        if dx == 2:
-            for way in range(2):
-                go(do_copy(way))
-            forward_weights(0)
-        elif dx:
-            way = step.index(dx)
-            go(dn_copy(way, 1 - way))
-    forward_weights(1)
-    for way in range(2):
-        do_copy(way).wait_recv()
-        xx = xpeer(step[way])
-        dkv[xx, way] = (dkv[xx, way].astype(F32) + dkv_o[way].astype(F32)).astype(BF16)
-        go(dn_copy(way, way))
-
-    for de in range(NE):
-        for dh in range(ND):
-            if de or dh:
-                tk_copy(de, dh).wait_recv()
-
-    @pl.loop(0, NE)
-    def _(i):
-        h = i // (NE // 2)
-        e = lax.rem(i, NE // 2) * 2
-        one = trecv[h, e].astype(F32)
-        two = trecv[h, e + 1].astype(F32)
-        at = pl.ds(pl.multiple_of(i * 2 * CAP, 2 * CAP), 2 * CAP)
-        gbuf[at, 0:PART] = jnp.concatenate([one[0:CAP], two[0:CAP]], axis=0).astype(BF16)
-        rest = jnp.concatenate([one[CAP:], two[CAP:]], axis=0).astype(BF16)
-        gbuf[at, PART:HALF] = rest[:, 0 : HALF - PART]
-        abuf[at] = rest[:, HALF - PART :]
+    def pair(h, other, j):
+        return (h * 2 + other) * 2 + j, lax.rem(exp + other, 2) + 4 * j
+
+    def unpack(other):
+        for de in range(NE):
+            for dh in range(ND):
+                if (de or dh) and de % 2 == other:
+                    tk_copy(de, dh).wait_recv()
+
+        @pl.loop(0, 2 * ND)
+        def _(i):
+            h = i // 2
+            slot, e = pair(h, other, lax.rem(i, 2))
+            one = trecv[h, e].astype(F32)
+            two = trecv[h, e + 2].astype(F32)
+            at = pl.ds(pl.multiple_of(slot * 2 * CAP, 2 * CAP), 2 * CAP)
+            gbuf[at, 0:PART] = jnp.concatenate([one[0:CAP], two[0:CAP]], axis=0).astype(BF16)
+            rest = jnp.concatenate([one[CAP:], two[CAP:]], axis=0).astype(BF16)
+            gbuf[at, PART:HALF] = rest[:, 0 : HALF - PART]
+            abuf[at] = rest[:, HALF - PART :]
 
     def go_copy(way, s):
         return remote(
@@ -459,38 +485,40 @@
             wg[at] = (wg[at].astype(F32) + theirs.astype(F32)).astype(BF16)
             go(gn_copy(way, s, way))
 
-    for i in range(HALF // FF):
-        at = slice(i * FF, (i + 1) * FF)
-        wg[at] = dot(gbuf[:, at], abuf[...], TN).astype(BF16)
-        if i == 2:
+    def weight_grads(chunks):
+        for i in chunks:
+            at = slice(i * FF, (i + 1) * FF)
+            wg[at] = dot(gbuf[:, at], abuf[...], TN).astype(BF16)
+
+    for dx in (2, 1, 3, 0):
+        xx = xpeer(dx)
+        if dx == 0:
+            for way in range(2):
+                do_copy(way).wait_recv()
+                to = xpeer(step[way])
+                dkv[to, way] = (dkv[to, way].astype(F32) + dkv_o[way].astype(F32)).astype(BF16)
+                go(dn_copy(way, way))
+            unpack(1)
+            weight_grads(range(3))
             send_grads(0)
+            weight_grads(range(3, HALF // FF))
+
+        @pl.loop(0, NZ)
+        def _(zz):
+            second_pass(xx, zz)
+
+        if dx == 2:
+            for way in range(2):
+                go(do_copy(way))
+            forward_weights(w_first)
+        elif dx:
+            way = step.index(dx)
+            go(dn_copy(way, 1 - way))
+            if dx == 1:
+                forward_weights(1 - w_first)
+                unpack(0)
+    join_grads(0)
     send_grads(1)
-    join_grads(0)
-
-    for s in range(2):
-        for way in range(2):
-            wf_copy(way, s, xpeer(2)).wait_recv()
-    hidden = dot(gbuf[...], wfull[...])
-    for h in range(ND):
-        for e in range(NE):
-            i = h * NE + e
-            hsend[h, e] = hidden[i * CAP : (i + 1) * CAP]
-
-    def hb_copy(de, dh):
-        e_to = lax.rem(exp + de, NE)
-        h_to = lax.rem(core + dh, ND)
-        i = de * ND + dh
-        return remote(
-            hsend.at[h_to, e_to], hrecv.at[core, exp], hb_s.at[i], hb_r.at[i], (ctx, e_to, h_to)
-        )
-
-    for de in range(NE):
-        for dh in range(ND):
-            if de == 0 and dh == 0:
-                hrecv[core, exp] = hsend[core, exp]
-            else:
-                go(hb_copy(de, dh))
-    join_grads(1)
 
     def dz_copy(dz):
         return remote(
@@ -515,10 +543,33 @@
 
     for dz in (2, 1, 3):
         go(dz_copy(dz))
-    for h in range(GROUP):
-        dq_out[:, h * HD : (h + 1) * HD] = (
-            jnp.transpose(dq_acc[:, h * QRY : (h + 1) * QRY]) * inv_root
-        ).astype(BF16)
+    for s in range(2):
+        for way in range(2):
+            wf_copy(way, s, xpeer(2)).wait_recv()
+    hidden = dot(gbuf[...], wfull[...])
+    for h in range(ND):
+        for other in range(2):
+            for j in range(2):
+                slot, e = pair(h, other, j)
+                for two in range(2):
+                    row = (slot * 2 + two) * CAP
+                    hsend[h, e + 2 * two] = hidden[row : row + CAP]
+
+    hx_copy = remote(
+        hsend.at[1 - core], hother, hx_s.at[0], hx_r.at[0], (ctx, exp, 1 - core)
+    )
+    go(hx_copy)
+
+    def hb_copy(de):
+        e_to = lax.rem(exp + de, NE)
+        return remote(hsum.at[e_to], hrecv.at[exp], hb_s.at[de], hb_r.at[de], (ctx, e_to, core))
+
+    hx_copy.wait_recv()
+    hsum[...] = hsend[core] + hother[...]
+    hrecv[exp] = hsum[exp]
+    for de in (1, 7, 3, 5, 4, 2, 6):
+        go(hb_copy(de))
+    join_grads(1)
 
     def gz_copy(s, h):
         return remote(
@@ -551,11 +602,15 @@
     wg_zs[:, :, WS:WP] = jnp.zeros((2, ND, WP - WS, FF), BF16)
     sum_grads(0)
 
-    for de in range(NE):
-        for dh in range(ND):
-            if de or dh:
-                hb_copy(de, dh).wait_recv()
-    back_rows = jnp.concatenate([hrecv[0, e] + hrecv[1, e] for e in range(NE)], axis=0)
+    sum_grads(1)
+    for h in range(GROUP):
+        dq_out[:, h * HD : (h + 1) * HD] = (
+            jnp.transpose(dq_acc[:, h * QRY : (h + 1) * QRY]) * inv_root
+        ).astype(BF16)
+
+    for de in range(1, NE):
+        hb_copy(de).wait_recv()
+    back_rows = jnp.concatenate([hrecv[e] for e in range(NE)], axis=0)
     high = back_rows.astype(BF16)
     low = (back_rows - high.astype(F32)).astype(BF16)
     mine = dot(perm[...], high, TN) + dot(perm[...], low, TN)
@@ -571,7 +626,6 @@
             sums = sums + dkv_zr[i, part].astype(F32)
         out[...] = sums.astype(BF16)
 
-    sum_grads(1)
     for zz in range(NZ):
 
         @pl.when(jnp.logical_not((zz == z) & (core == w_core)))
@@ -587,10 +641,21 @@
 
     for copy in sent:
         copy.wait_send()
+    for way in range(2):
+        for s in range(2):
+            wx_copy(way, s, x).wait_send()
 
     @pl.when(jnp.logical_not(w_here))
     def _():
         wz_copy(0).wait_send()
+
+    for way in range(2):
+        zz = zpeer(back[way])
+
+        @pl.when(core == zz // 2)
+        def _():
+            for h in range(ND):
+                wf_zcopy(way, zz, h).wait_send()
 
     for s in range(2):
         for h in range(ND):
@@ -651,13 +716,17 @@
         pltpu.VMEM((2, ND, WP, FF), BF16),
         pltpu.VMEM((NZ, WP, FF), BF16),
         pltpu.VMEM((ND, NE, CAP, FF), F32),
-        pltpu.VMEM((ND, NE, CAP, FF), F32),
+        pltpu.VMEM((NE, CAP, FF), F32),
+        pltpu.VMEM((NE, CAP, FF), F32),
+        pltpu.VMEM((NE, CAP, FF), F32),
     ]
     for size in (
-        NZ - 1,
+        2,
+        2,
         2 * NZ,
         2 * NZ,
         NZ,
+        4,
         4,
         4,
         NE * ND,
@@ -667,7 +736,8 @@
         4,
         8,
         NZ,
-        NE * ND,
+        1,
+        NE,
     ):
         scratch += [dma((size,)), dma((size,))]
     shapes = (

time: 164 us -> 149 us (0.909); the launches traced: 164 us -> 146 us
  Pallas kernels: 163 us -> 146 us
    pallas_call x1, Pallas kernels: 161 us -> 144 us  [per_device(): pl.pallas_call(kernel, name='layer_backward', out_shape=shapes, in_specs=...]
where the time goes in v3:
time: 149 us; the launch traced here: 146 us
  Pallas kernels  146 us (98%)
    pallas_call x1, Pallas kernels, per_device(): pl.pallas_call(kernel, name='layer_backward', out_shape=shapes, in_specs=...  144 us

profile of v3, /device:TPU:81, one launch (start us, length us, event | category | flops | bytes accessed | tf_op | source)
XLA Modules:
  0.0 146.4 jit_solution(13847736354102296782)
XLA Ops:
  0.6 143.6 %layer_backward.1 = (bf16[128,1280]{1,0:T(8,128)(2,1)}, bf16[256,128]{1,0:T(8,128)(2,1)}, bf16[256,128]{1,0:T(8,128)(2,1)}, bf16[128,640]{1,0:T(8,128)(2,1)}, bf...) custom-call(s32[16]{0:T(128)} %off_ref.1, bf16[128,1280]{1,0:T(8,128)(2,1)} %bitcast.12, bf16[256,128]{1,0:T(8,128)(2,1)} %bitcast.15, ...), custom_call_target="tpu_custom_call" | custom-call | tf_op jit(solution)/shard_map/layer_backward/pallas_call | solution.py:751
  144.3 2.1 %finish.1 = (bf16[128,1280]{1,0:T(8,128)(2,1)}, bf16[256,128]{1,0:T(8,128)(2,1)}, bf16[256,128]{1,0:T(8,128)(2,1)}, bf16[128,640]{1,0:T(8,128)(2,1)}, bf16[1,128]{1,0:T(2,128)(2,1)}, /*index=5*/bf16[200,640]{1,0:T(8,128)(2,1)}) custom-call(bf16[128,1280]{1,0:T(8,128)(2,1)} %get-tuple-element.18.refs_0_, bf16[256,128]{1,0:T(8,128)(2,1)} %get-tuple-element.19.refs_1_, ...), custom_call_target="tpu_custom_call" | custom-call | tf_op jit(solution)/shard_map/finish/pallas_call | solution.py:773

commit v4 on v3

--- a/solution.py
+++ b/solution.py
@@ -205,8 +205,6 @@
             (zpeer(dz) * NX + x, exp, w_core),
         )
 
-    for dz in step:
-        go(wz_copy(dz))
 
     @pl.when(w_here)
     def _():
@@ -301,6 +299,8 @@
         wz_wait(w_slot, 1 - core)
         place_weights(w_slot)
 
+    for dz in step:
+        go(wz_copy(dz))
     trecv[core, exp] = tsend[core, exp]
     go(tk_copy(0, 1))
     for de in (4, 2, 6):
@@ -313,6 +313,14 @@
         go(kg_copy(way, zz))
         for to in range(2):
             go(kx_copy(to, back[1 - way], x))
+
+    def forward_keys(dz):
+        for way in range(2):
+            xx = xpeer(back[way])
+            kx_copy(way, dz, xx).wait_recv()
+            go(kf_copy(way, dz, xx))
+
+    forward_keys(0)
     for way in range(2):
         zz = zpeer(back[way])
 
@@ -326,17 +334,15 @@
         kg_copy(way, zpeer(2)).wait_recv()
     for way in range(2):
         go(kx_copy(way, 2, x))
+    forward_keys(1)
+    forward_keys(3)
     place_weights(w_other)
 
     for h in range(GROUP):
         qs[h * QRY : (h + 1) * QRY] = q_ref[:, h * HD : (h + 1) * HD]
         dos[h * QRY : (h + 1) * QRY] = do_ref[:, h * HD : (h + 1) * HD]
 
-    for dz in (0, 1, 3, 2):
-        for way in range(2):
-            xx = xpeer(back[way])
-            kx_copy(way, dz, xx).wait_recv()
-            go(kf_copy(way, dz, xx))
+    forward_keys(2)
 
     own_pos = off_ref[ctx] * KEYS + (KEYS - QRY)
     q_pos = own_pos + lax.broadcasted_iota(jnp.int32, (KEYS, QRY), 1)
@@ -396,6 +402,8 @@
         def _(zz):
             first_pass(xx, zz)
 
+        if dx == 1:
+            forward_weights(w_first)
     total = stat_l[...]
     stat_m[...] = stat_m[...] + jnp.log2(total)
     stat_d[...] = stat_d[...] / total
@@ -452,38 +460,43 @@
             gbuf[at, PART:HALF] = rest[:, 0 : HALF - PART]
             abuf[at] = rest[:, HALF - PART :]
 
-    def go_copy(way, s):
+    g_cols = (pl.ds(0, 3 * HD), pl.ds(3 * HD, FF - 3 * HD))
+
+    def go_copy(way, s, c):
+        i = (way * 2 + s) * 2 + c
         return remote(
-            wg.at[w_rows(xpeer(2), s, way)],
-            (wg_oa, wg_ob)[way].at[s],
-            go_s.at[way * 2 + s],
-            go_r.at[way * 2 + s],
+            wg.at[w_rows(xpeer(2), s, way), g_cols[c]],
+            (wg_oa, wg_ob)[way].at[s, :, g_cols[c]],
+            go_s.at[i],
+            go_r.at[i],
             near[way],
         )
 
-    def gn_copy(way, s, part):
-        i = (way * 2 + s) * 2 + part
+    def gn_copy(way, s, part, c):
+        i = ((way * 2 + s) * 2 + part) * 2 + c
         return remote(
-            wg.at[w_rows(xpeer(step[way]), s, part)],
-            wg_n.at[way, s, pl.ds(w_halves[part][0], w_halves[part][1])],
+            wg.at[w_rows(xpeer(step[way]), s, part), g_cols[c]],
+            wg_n.at[way, s, pl.ds(w_halves[part][0], w_halves[part][1]), g_cols[c]],
             gn_s.at[i],
             gn_r.at[i],
             near[way],
         )
 
-    def send_grads(s):
+    def send_far(s, c):
         for way in range(2):
-            go(go_copy(way, s))
+            go(go_copy(way, s, c))
+
+    def send_near(s, c):
         for way in range(2):
-            go(gn_copy(way, s, 1 - way))
-
-    def join_grads(s):
+            go(gn_copy(way, s, 1 - way, c))
+
+    def join_grads(s, c):
         for way in range(2):
-            go_copy(way, s).wait_recv()
+            go_copy(way, s, c).wait_recv()
             at = w_rows(xpeer(step[way]), s, way)
-            theirs = (wg_oa, wg_ob)[way][s]
-            wg[at] = (wg[at].astype(F32) + theirs.astype(F32)).astype(BF16)
-            go(gn_copy(way, s, way))
+            theirs = (wg_oa, wg_ob)[way][s, :, g_cols[c]]
+            wg[at, g_cols[c]] = (wg[at, g_cols[c]].astype(F32) + theirs.astype(F32)).astype(BF16)
+            go(gn_copy(way, s, way, c))
 
     def weight_grads(chunks):
         for i in chunks:
@@ -500,7 +513,9 @@
                 go(dn_copy(way, way))
             unpack(1)
             weight_grads(range(3))
-            send_grads(0)
+            for c in range(2):
+                send_far(0, c)
+                send_near(0, c)
             weight_grads(range(3, HALF // FF))
 
         @pl.loop(0, NZ)
@@ -510,15 +525,17 @@
         if dx == 2:
             for way in range(2):
                 go(do_copy(way))
-            forward_weights(w_first)
+            forward_weights(1 - w_first)
         elif dx:
             way = step.index(dx)
             go(dn_copy(way, 1 - way))
             if dx == 1:
-                forward_weights(1 - w_first)
                 unpack(0)
-    join_grads(0)
-    send_grads(1)
+    join_grads(0, 0)
+    join_grads(0, 1)
+    send_far(1, 0)
+    send_near(1, 0)
+    send_far(1, 1)
 
     def dz_copy(dz):
         return remote(
@@ -564,45 +581,50 @@
         e_to = lax.rem(exp + de, NE)
         return remote(hsum.at[e_to], hrecv.at[exp], hb_s.at[de], hb_r.at[de], (ctx, e_to, core))
 
+    join_grads(1, 0)
+    send_near(1, 1)
+
+
+    def gz_copy(s, h, c):
+        i = (s * 2 + h) * 2 + c
+        return remote(
+            wg_zs.at[s, h, :, g_cols[c]],
+            wg_zr.at[z, :, g_cols[c]],
+            gz_s.at[i],
+            gz_r.at[z * 2 + c],
+            ((2 * core + s) * NX + x, exp, h),
+        )
+
+    def sum_grads(s, c):
+        for way in range(2):
+            for part in range(2):
+                gn_copy(way, s, part, c).wait_recv()
+        sums = wg[w_rows(x, s), g_cols[c]].astype(F32)
+        for way in range(2):
+            sums = sums + wg_n[way, s, :, g_cols[c]].astype(F32)
+        for h in range(ND):
+            wg_zs[s, h, 0:WS, g_cols[c]] = sums[h * WS : (h + 1) * WS].astype(BF16)
+            own = (2 * core + s == z) & (core == h)
+
+            @pl.when(own)
+            def _():
+                wg_zr[z, :, g_cols[c]] = wg_zs[s, h, :, g_cols[c]]
+
+            @pl.when(jnp.logical_not(own))
+            def _():
+                gz_copy(s, h, c).start()
+
+    wg_zs[:, :, WS:WP] = jnp.zeros((2, ND, WP - WS, FF), BF16)
+    sum_grads(0, 0)
+    sum_grads(0, 1)
     hx_copy.wait_recv()
     hsum[...] = hsend[core] + hother[...]
     hrecv[exp] = hsum[exp]
     for de in (1, 7, 3, 5, 4, 2, 6):
         go(hb_copy(de))
-    join_grads(1)
-
-    def gz_copy(s, h):
-        return remote(
-            wg_zs.at[s, h],
-            wg_zr.at[z],
-            gz_s.at[s * 2 + h],
-            gz_r.at[z],
-            ((2 * core + s) * NX + x, exp, h),
-        )
-
-    def sum_grads(s):
-        for way in range(2):
-            for part in range(2):
-                gn_copy(way, s, part).wait_recv()
-        sums = wg[w_rows(x, s)].astype(F32)
-        for way in range(2):
-            sums = sums + wg_n[way, s].astype(F32)
-        for h in range(ND):
-            wg_zs[s, h, 0:WS] = sums[h * WS : (h + 1) * WS].astype(BF16)
-            own = (2 * core + s == z) & (core == h)
-
-            @pl.when(own)
-            def _():
-                wg_zr[z] = wg_zs[s, h]
-
-            @pl.when(jnp.logical_not(own))
-            def _():
-                gz_copy(s, h).start()
-
-    wg_zs[:, :, WS:WP] = jnp.zeros((2, ND, WP - WS, FF), BF16)
-    sum_grads(0)
-
-    sum_grads(1)
+    join_grads(1, 1)
+    sum_grads(1, 0)
+    sum_grads(1, 1)
     for h in range(GROUP):
         dq_out[:, h * HD : (h + 1) * HD] = (
             jnp.transpose(dq_acc[:, h * QRY : (h + 1) * QRY]) * inv_root
@@ -626,18 +648,23 @@
             sums = sums + dkv_zr[i, part].astype(F32)
         out[...] = sums.astype(BF16)
 
-    for zz in range(NZ):
-
-        @pl.when(jnp.logical_not((zz == z) & (core == w_core)))
-        def _():
-            remote(
-                wg_zs.at[0, 0], wg_zr.at[zz], gz_s.at[0], gz_r.at[zz], (ctx, exp, core)
-            ).wait_recv()
-
-    sums = wg_zr[0].astype(F32)
-    for zz in range(1, NZ):
-        sums = sums + wg_zr[zz].astype(F32)
-    dw_out[...] = sums[0:WS].astype(BF16)
+    for c in range(2):
+        for zz in range(NZ):
+
+            @pl.when(jnp.logical_not((zz == z) & (core == w_core)))
+            def _():
+                remote(
+                    wg_zs.at[0, 0, :, g_cols[c]],
+                    wg_zr.at[zz, :, g_cols[c]],
+                    gz_s.at[0],
+                    gz_r.at[zz * 2 + c],
+                    (ctx, exp, core),
+                ).wait_recv()
+
+        sums = wg_zr[0, :, g_cols[c]].astype(F32)
+        for zz in range(1, NZ):
+            sums = sums + wg_zr[zz, :, g_cols[c]].astype(F32)
+        dw_out[:, g_cols[c]] = sums[0:WS].astype(BF16)
 
     for copy in sent:
         copy.wait_send()
@@ -662,7 +689,8 @@
 
             @pl.when(jnp.logical_not((2 * core + s == z) & (core == h)))
             def _():
-                gz_copy(s, h).wait_send()
+                for c in range(2):
+                    gz_copy(s, h, c).wait_send()
 
 
 def finish(*refs):
@@ -733,9 +761,9 @@
         2,
         4,
         NZ - 1,
-        4,
         8,
-        NZ,
+        16,
+        8,
         1,
         NE,
     ):

time: 149 us -> 146 us (0.980); the launches traced: 146 us -> 146 us
  no operation moved by 1% of the time
where the time goes in v4:
time: 146 us
  Pallas kernels  145 us (99%)
    pallas_call x1, Pallas kernels, per_device(): pl.pallas_call(kernel, name='layer_backward', out_shape=shapes, in_specs=...  143 us

profile of v4, /device:TPU:81, one launch (start us, length us, event | category | flops | bytes accessed | tf_op | source)
XLA Modules:
  0.0 145.6 jit_solution(2246994373337861058)
XLA Ops:
  0.6 142.9 %layer_backward.1 = (bf16[128,1280]{1,0:T(8,128)(2,1)}, bf16[256,128]{1,0:T(8,128)(2,1)}, bf16[256,128]{1,0:T(8,128)(2,1)}, bf16[128,640]{1,0:T(8,128)(2,1)}, bf...) custom-call(s32[16]{0:T(128)} %off_ref.1, bf16[128,1280]{1,0:T(8,128)(2,1)} %bitcast.12, bf16[256,128]{1,0:T(8,128)(2,1)} %bitcast.15, ...), custom_call_target="tpu_custom_call" | custom-call | tf_op jit(solution)/shard_map/layer_backward/pallas_call | solution.py:779
  143.5 2.1 %finish.1 = (bf16[128,1280]{1,0:T(8,128)(2,1)}, bf16[256,128]{1,0:T(8,128)(2,1)}, bf16[256,128]{1,0:T(8,128)(2,1)}, bf16[128,640]{1,0:T(8,128)(2,1)}, bf16[1,128]{1,0:T(2,128)(2,1)}, /*index=5*/bf16[200,640]{1,0:T(8,128)(2,1)}) custom-call(bf16[128,1280]{1,0:T(8,128)(2,1)} %get-tuple-element.18.refs_0_, bf16[256,128]{1,0:T(8,128)(2,1)} %get-tuple-element.19.refs_1_, ...), custom_call_target="tpu_custom_call" | custom-call | tf_op jit(solution)/shard_map/finish/pallas_call | solution.py:801

commit v5 on v4

--- a/solution.py
+++ b/solution.py
@@ -251,6 +251,44 @@
     w_other = lax.rem(z + 1, 2)
     w_first = lax.rem(z + (core - w_core) * (core - w_core), 2)
 
+    @pl.when(w_here)
+    def _():
+        wz_wait(w_slot, 1 - core)
+        place_weights(w_slot)
+
+    for dz in step:
+        go(wz_copy(dz))
+    for way in range(2):
+        zz = zpeer(back[way])
+        kz_copy(way, zz).wait_recv()
+        go(kg_copy(way, zz))
+        for to in range(2):
+            go(kx_copy(to, back[1 - way], x))
+
+    def forward_keys(dz):
+        for way in range(2):
+            xx = xpeer(back[way])
+            kx_copy(way, dz, xx).wait_recv()
+            go(kf_copy(way, dz, xx))
+
+    forward_keys(0)
+    for way in range(2):
+        zz = zpeer(back[way])
+
+        @pl.when(core == zz // 2)
+        def _():
+            for h in range(ND):
+                wz_wait(lax.rem(zz, 2), h)
+                wf_zcopy(way, zz, h).start()
+
+    for way in range(2):
+        kg_copy(way, zpeer(2)).wait_recv()
+    for way in range(2):
+        go(kx_copy(way, 2, x))
+    forward_keys(1)
+    forward_keys(3)
+    place_weights(w_other)
+
     row_at = lax.broadcasted_iota(jnp.int32, (TOK, TOK), 0)
     col_at = lax.broadcasted_iota(jnp.int32, (TOK, TOK), 1)
     eye = row_at == col_at
@@ -294,49 +332,12 @@
                 [first[rows, HALF - PART : PART], third[rows]], axis=0
             ).astype(BF16)
 
-    @pl.when(w_here)
-    def _():
-        wz_wait(w_slot, 1 - core)
-        place_weights(w_slot)
-
-    for dz in step:
-        go(wz_copy(dz))
     trecv[core, exp] = tsend[core, exp]
     go(tk_copy(0, 1))
     for de in (4, 2, 6):
         for dh in range(ND):
             go(tk_copy(de, dh))
 
-    for way in range(2):
-        zz = zpeer(back[way])
-        kz_copy(way, zz).wait_recv()
-        go(kg_copy(way, zz))
-        for to in range(2):
-            go(kx_copy(to, back[1 - way], x))
-
-    def forward_keys(dz):
-        for way in range(2):
-            xx = xpeer(back[way])
-            kx_copy(way, dz, xx).wait_recv()
-            go(kf_copy(way, dz, xx))
-
-    forward_keys(0)
-    for way in range(2):
-        zz = zpeer(back[way])
-
-        @pl.when(core == zz // 2)
-        def _():
-            for h in range(ND):
-                wz_wait(lax.rem(zz, 2), h)
-                wf_zcopy(way, zz, h).start()
-
-    for way in range(2):
-        kg_copy(way, zpeer(2)).wait_recv()
-    for way in range(2):
-        go(kx_copy(way, 2, x))
-    forward_keys(1)
-    forward_keys(3)
-    place_weights(w_other)
 
     for h in range(GROUP):
         qs[h * QRY : (h + 1) * QRY] = q_ref[:, h * HD : (h + 1) * HD]

time: 146 us -> 146 us (level)
  no operation moved by 1% of the time
where the time goes in v5:
time: 146 us
  Pallas kernels  145 us (99%)
    pallas_call x1, Pallas kernels, per_device(): pl.pallas_call(kernel, name='layer_backward', out_shape=shapes, in_specs=...  143 us

profile of v5, /device:TPU:81, one launch (start us, length us, event | category | flops | bytes accessed | tf_op | source)
XLA Modules:
  0.0 145.6 jit_solution(13863619186238630098)
XLA Ops:
  0.6 142.9 %layer_backward.1 = (bf16[128,1280]{1,0:T(8,128)(2,1)}, bf16[256,128]{1,0:T(8,128)(2,1)}, bf16[256,128]{1,0:T(8,128)(2,1)}, bf16[128,640]{1,0:T(8,128)(2,1)}, bf...) custom-call(s32[16]{0:T(128)} %off_ref.1, bf16[128,1280]{1,0:T(8,128)(2,1)} %bitcast.12, bf16[256,128]{1,0:T(8,128)(2,1)} %bitcast.15, ...), custom_call_target="tpu_custom_call" | custom-call | tf_op jit(solution)/shard_map/layer_backward/pallas_call | solution.py:780
  143.5 2.1 %finish.1 = (bf16[128,1280]{1,0:T(8,128)(2,1)}, bf16[256,128]{1,0:T(8,128)(2,1)}, bf16[256,128]{1,0:T(8,128)(2,1)}, bf16[128,640]{1,0:T(8,128)(2,1)}, bf16[1,128]{1,0:T(2,128)(2,1)}, /*index=5*/bf16[200,640]{1,0:T(8,128)(2,1)}) custom-call(bf16[128,1280]{1,0:T(8,128)(2,1)} %get-tuple-element.18.refs_0_, bf16[256,128]{1,0:T(8,128)(2,1)} %get-tuple-element.19.refs_1_, ...), custom_call_target="tpu_custom_call" | custom-call | tf_op jit(solution)/shard_map/finish/pallas_call | solution.py:802
